TPU v7x, 32 devices: a whole 2x2x4 slice. The times are simulated.
32 devices in a mesh: dp: 16 (over z, y, core), tensor: 2 (over x).
Axes of the slice: x: 2, y: 2, z: 4, core: 2. Of those that a mesh axis runs over, the one named last changes fastest.
Arguments:
- tokens: bfloat16 [32768, 768], P('dp'), may hold values from -6 to 6
- cotangent: bfloat16 [32768, 768], P('dp'), may hold values from -6 to 6
- pair_lengths: int32 [64, 4], P('dp'), may hold values from 1 to 256, 512 in all within a row
- block_of_slot: int32 [224], replicated, may hold values from 0 to 216, as said below
- masters: float32 [2, 224, 128, 128], P('tensor', 'dp'), may hold values from -4 to 4
- mom_first: float32 [2, 224, 128, 128], P('tensor', 'dp'), may hold values from -0.078125 to 0.078125
- mom_second: float32 [2, 224, 128, 128], P('tensor', 'dp'), may hold values from 3.0517579e-06 to 6.1035156e-05
- left_bases: float32 [2, 224, 128, 128], P('tensor', 'dp'), may hold values from -1 to 1, as said below
- right_bases: float32 [2, 224, 128, 128], P('tensor', 'dp'), may hold values from -1 to 1, as said below
- split_vec: float32 [2, 2304], P('tensor'), may hold values from -4 to 4
- split_first: float32 [2, 2304], P('tensor'), may hold values from -0.078125 to 0.078125
- split_second: float32 [2, 2304], P('tensor'), may hold values from 3.0517579e-06 to 6.1035156e-05
- row_vec: float32 [6, 768], replicated, may hold values from -2 to 2
- row_first: float32 [6, 768], replicated, may hold values from -0.078125 to 0.078125
- row_second: float32 [6, 768], replicated, may hold values from 3.0517579e-06 to 6.1035156e-05
Outputs:
- layer_out: bfloat16 [32768, 768], P('dp')
- input_grad: float32 [32768, 768], P('dp')
- weight_grads: float32 [2, 224, 128, 128], P('tensor', 'dp')
- new_masters: float32 [2, 224, 128, 128], P('tensor', 'dp')
- new_first: float32 [2, 224, 128, 128], P('tensor', 'dp')
- new_second: float32 [2, 224, 128, 128], P('tensor', 'dp')
- weight_copies: bfloat16 [2, 224, 128, 128], P('tensor', 'dp')
- split_grad: float32 [2, 2304], P('tensor')
- new_split: float32 [2, 2304], P('tensor')
- new_split_first: float32 [2, 2304], P('tensor')
- new_split_second: float32 [2, 2304], P('tensor')
- row_grad: float32 [6, 768], replicated
- new_row: float32 [6, 768], replicated
- new_row_first: float32 [6, 768], replicated
- new_row_second: float32 [6, 768], replicated
Inputs may be any that keep to these rules, and one draw needn't show every extreme that they name: `block_of_slot`: each block number 0 to 215 stands in exactly one slot and 216 marks an empty slot; index d of dp owns slots d * 14 to (d + 1) * 14 - 1. `left_bases`: each [128, 128] matrix is orthogonal. `right_bases`: each [128, 128] matrix is orthogonal.
All inputs are finite; a program needn't handle non-finite values.
Results may differ from a plain program's by a relative error of at most 0.018.
Values may be sent and summed in bfloat16 or wider, within the bound.
A program may use at most 192 MiB of HBM per device.

v0:
```python
import jax
import jax.numpy as jnp
from jax import lax
from jax.sharding import PartitionSpec as P

D = 768
HEADS = 12
HEAD = 64
FF = 3072


EPS_NORM = 1e-05
EPS_ADAM = 1e-08
LEARN_RATE = 0.01
VECTOR_RATE = 0.15
MOMENT_DECAY = 0.5
MASKED_SCORE = -1e30
HIGHEST_PRECISION = lax.Precision.HIGHEST


def norm_row(hidden, gain_vec, shift_vec):
    row_mean = jnp.mean(hidden, axis=-1, keepdims=True)
    centred = hidden - row_mean
    row_var = jnp.mean(centred * centred, axis=-1, keepdims=True)
    return centred * lax.rsqrt(row_var + EPS_NORM) * gain_vec + shift_vec


def gelu_exact(operand):
    return jax.nn.gelu(operand, approximate=False)


def segment_ids(pair_sizes, seq_len):
    pair_ends = jnp.cumsum(pair_sizes, axis=-1)
    position = jnp.arange(seq_len, dtype=jnp.int32)
    hits = (position[None, :, None] >= pair_ends[:, None, :-1]).astype(jnp.int32)
    return jnp.sum(hits, axis=-1)


def slot_table(block_of_slot, block_total):
    slot_numbers = jnp.arange(block_of_slot.shape[0], dtype=jnp.int32)
    matches = block_of_slot[:, None] == jnp.arange(block_total, dtype=jnp.int32)[None, :]
    return jnp.sum(jnp.where(matches, slot_numbers[:, None], 0), axis=0)


def to_blocks(matrix, block_edge):
    row_total, col_total = matrix.shape
    shaped = matrix.reshape(
        row_total // block_edge, block_edge, col_total // block_edge, block_edge
    )
    return shaped.transpose(0, 2, 1, 3).reshape(-1, block_edge, block_edge)


def from_blocks(blocks, row_total, col_total):
    block_edge = blocks.shape[-1]
    shaped = blocks.reshape(
        row_total // block_edge, col_total // block_edge, block_edge, block_edge
    )
    return shaped.transpose(0, 2, 1, 3).reshape(row_total, col_total)


def block_counts(block_edge, head_width, ffn_width):
    return (
        D // block_edge * (3 * head_width // block_edge),
        head_width // block_edge * (D // block_edge),
        D // block_edge * (ffn_width // block_edge),
        ffn_width // block_edge * (D // block_edge),
    )


def unpack(blocks, block_edge, head_width, ffn_width):
    counts_list = block_counts(block_edge, head_width, ffn_width)
    first_end = counts_list[0]
    second_end = first_end + counts_list[1]
    third_end = second_end + counts_list[2]
    fourth_end = third_end + counts_list[3]
    return (
        from_blocks(blocks[:first_end], D, 3 * head_width),
        from_blocks(blocks[first_end:second_end], head_width, D),
        from_blocks(blocks[second_end:third_end], D, ffn_width),
        from_blocks(blocks[third_end:fourth_end], ffn_width, D),
    )


def pack(qkv_matrix, out_matrix, up_matrix, down_matrix, block_edge):
    return jnp.concatenate(
        [
            to_blocks(qkv_matrix, block_edge),
            to_blocks(out_matrix, block_edge),
            to_blocks(up_matrix, block_edge),
            to_blocks(down_matrix, block_edge),
        ],
        axis=0,
    )


def rotate_update(gradient, moment_one, moment_two, left, right, master):
    turned = jnp.einsum("psji,psjk->psik", left, gradient, precision=HIGHEST_PRECISION)
    turned = jnp.einsum("psik,pskl->psil", turned, right, precision=HIGHEST_PRECISION)
    first_new = MOMENT_DECAY * moment_one + (1.0 - MOMENT_DECAY) * turned
    second_new = MOMENT_DECAY * moment_two + (1.0 - MOMENT_DECAY) * turned * turned
    stepped = first_new / (jnp.sqrt(second_new) + EPS_ADAM)
    turned_back = jnp.einsum("psij,psjk->psik", left, stepped, precision=HIGHEST_PRECISION)
    turned_back = jnp.einsum("psik,pslk->psil", turned_back, right, precision=HIGHEST_PRECISION)
    return (master - LEARN_RATE * turned_back, first_new, second_new)


def adam_vector(gradient, moment_one, moment_two, current):
    first_new = MOMENT_DECAY * moment_one + (1.0 - MOMENT_DECAY) * gradient
    second_new = MOMENT_DECAY * moment_two + (1.0 - MOMENT_DECAY) * gradient * gradient
    return (
        current - VECTOR_RATE * first_new / (jnp.sqrt(second_new) + EPS_ADAM),
        first_new,
        second_new,
    )


def masked_scores(query_row, key_row, seg_row):
    raw_scores = jnp.einsum(
        "qhd,khd->hqk", query_row, key_row, preferred_element_type=jnp.float32
    ) * HEAD ** (-0.5)
    same_pair = seg_row[:, None] == seg_row[None, :]
    return jnp.where(same_pair[None], raw_scores, MASKED_SCORE)


def split_heads(matrix, row_count, seq_len, local_heads):
    return matrix.reshape(row_count, seq_len, local_heads, HEAD)


def body(
    tokens,
    cotangent,
    pair_lengths,
    block_of_slot,
    masters,
    mom_first,
    mom_second,
    left_bases,
    right_bases,
    split_vec,
    split_first,
    split_second,
    row_vec,
    row_first,
    row_second,
):
    pieces = lax.axis_size("tensor")
    piece_width = HEADS * HEAD // pieces
    piece_ffn = FF // pieces
    block_edge = masters.shape[-1]
    counts_list = block_counts(block_edge, piece_width, piece_ffn)
    block_total = counts_list[0] + counts_list[1] + counts_list[2] + counts_list[3]
    full_seq = tokens.shape[0] // pair_lengths.shape[0]
    everyone = lax.all_gather(masters.astype(jnp.bfloat16), "dp", axis=1, tiled=True)
    slot_of = slot_table(block_of_slot, block_total)
    local_heads = HEADS // pieces
    piece_count = everyone.shape[0]
    head_width = local_heads * HEAD
    unpacked = [unpack(jnp.take(everyone[0], slot_of, axis=0), block_edge, piece_width, piece_ffn)]
    w_qkv = jnp.concatenate(
        [
            jnp.concatenate(
                [
                    one_piece[0][:, part_index * piece_width : (part_index + 1) * piece_width]
                    for one_piece in unpacked
                ],
                axis=1,
            )
            for part_index in range(3)
        ],
        axis=1,
    )
    w_out = jnp.concatenate([one_piece[1] for one_piece in unpacked], axis=0)
    w_up = jnp.concatenate([one_piece[2] for one_piece in unpacked], axis=1)
    w_down = jnp.concatenate([one_piece[3] for one_piece in unpacked], axis=0)
    query_bias = split_vec[0][:piece_width]
    value_bias = split_vec[0][piece_width : 2 * piece_width]
    up_bias = split_vec[0][2 * piece_width :]
    out_bias, gain_one, shift_one, down_bias, gain_two, shift_two = (
        row_vec[row_number] for row_number in range(6)
    )
    token_count = tokens.shape[0]
    row_count = pair_lengths.shape[0]
    seg_rows = segment_ids(pair_lengths, full_seq)
    inputs = tokens.astype(jnp.float32)
    projected = jnp.dot(tokens, w_qkv, preferred_element_type=jnp.float32)
    queries = (projected[:, :head_width] + query_bias).astype(jnp.bfloat16)
    keys_proj = projected[:, head_width : 2 * head_width].astype(jnp.bfloat16)
    values = (projected[:, 2 * head_width :] + value_bias).astype(jnp.bfloat16)
    query_rows = split_heads(queries, row_count, full_seq, local_heads)
    key_rows = split_heads(keys_proj, row_count, full_seq, local_heads)
    value_rows = split_heads(values, row_count, full_seq, local_heads)

    def forward_row(row_items):
        query_row, key_row, value_row, seg_row = row_items
        scores = masked_scores(query_row, key_row, seg_row)
        row_top = jnp.max(scores, axis=-1, keepdims=True)
        log_total = row_top + jnp.log(jnp.sum(jnp.exp(scores - row_top), axis=-1, keepdims=True))
        probabilities = jnp.exp(scores - log_total)
        mixed = jnp.einsum(
            "hqk,khd->qhd",
            probabilities.astype(jnp.bfloat16),
            value_row,
            preferred_element_type=jnp.float32,
        )
        return (mixed.astype(jnp.bfloat16), log_total)

    mapped = lax.map(forward_row, (query_rows, key_rows, value_rows, seg_rows))
    attended = mapped[0].reshape(token_count, head_width)
    attn_part = jnp.dot(attended, w_out, preferred_element_type=jnp.float32)
    attn_sum = lax.psum(attn_part.astype(jnp.bfloat16), "tensor").astype(jnp.float32)
    hidden_one = inputs + attn_sum + out_bias
    normed_one, norm_one_back = jax.vjp(norm_row, hidden_one, gain_one, shift_one)
    normed_low = normed_one.astype(jnp.bfloat16)
    up_pre = jnp.dot(normed_low, w_up, preferred_element_type=jnp.float32) + up_bias
    active, gelu_back = jax.vjp(gelu_exact, up_pre)
    active_low = active.astype(jnp.bfloat16)
    down_part = jnp.dot(active_low, w_down, preferred_element_type=jnp.float32)
    down_sum = lax.psum(down_part.astype(jnp.bfloat16), "tensor").astype(jnp.float32)
    hidden_two = normed_one + down_sum + down_bias
    output, norm_two_back = jax.vjp(norm_row, hidden_two, gain_two, shift_two)
    layer_out = output.astype(jnp.bfloat16)
    grad_two, gain_two_grad, shift_two_grad = norm_two_back(cotangent.astype(jnp.float32))
    down_low = grad_two.astype(jnp.bfloat16)
    down_bias_grad = jnp.sum(grad_two, axis=0)
    down_weight_grad = jnp.dot(active_low.T, down_low, preferred_element_type=jnp.float32)
    grad_active = jnp.dot(down_low, w_down.T, preferred_element_type=jnp.float32)
    up_low = gelu_back(grad_active)[0].astype(jnp.bfloat16)
    up_bias_grad = jnp.sum(up_low.astype(jnp.float32), axis=0)
    up_weight_grad = jnp.dot(normed_low.T, up_low, preferred_element_type=jnp.float32)
    back_part = jnp.dot(up_low, w_up.T, preferred_element_type=jnp.float32)
    back_sum = lax.psum(back_part.astype(jnp.bfloat16), "tensor").astype(jnp.float32)
    grad_normed = grad_two + back_sum
    grad_one, gain_one_grad, shift_one_grad = norm_one_back(grad_normed)
    out_bias_grad = jnp.sum(grad_one, axis=0)
    attn_low = grad_one.astype(jnp.bfloat16)
    out_weight_grad = jnp.dot(attended.T, attn_low, preferred_element_type=jnp.float32)
    mixed_low = jnp.dot(attn_low, w_out.T, preferred_element_type=jnp.float32).astype(jnp.bfloat16)
    grad_rows = split_heads(mixed_low, row_count, full_seq, local_heads)

    def backward_row(row_items):
        query_row, key_row, value_row, seg_row, grad_row, log_total = row_items
        probabilities = jnp.exp(masked_scores(query_row, key_row, seg_row) - log_total)
        grad_probs = jnp.einsum(
            "qhd,khd->hqk", grad_row, value_row, preferred_element_type=jnp.float32
        )
        value_grad = jnp.einsum(
            "hqk,qhd->khd",
            probabilities.astype(jnp.bfloat16),
            grad_row,
            preferred_element_type=jnp.float32,
        )
        spread = jnp.sum(probabilities * grad_probs, axis=-1, keepdims=True)
        score_low = (probabilities * (grad_probs - spread)).astype(jnp.bfloat16)
        query_grad = jnp.einsum(
            "hqk,khd->qhd", score_low, key_row, preferred_element_type=jnp.float32
        ) * HEAD ** (-0.5)
        key_grad = jnp.einsum(
            "hqk,qhd->khd", score_low, query_row, preferred_element_type=jnp.float32
        ) * HEAD ** (-0.5)
        return (
            query_grad.astype(jnp.bfloat16),
            key_grad.astype(jnp.bfloat16),
            value_grad.astype(jnp.bfloat16),
        )

    saved_rows = mapped[1]
    query_low, key_low, value_low = lax.map(
        backward_row, (query_rows, key_rows, value_rows, seg_rows, grad_rows, saved_rows)
    )
    merged = jnp.concatenate(
        [
            query_low.reshape(token_count, head_width),
            key_low.reshape(token_count, head_width),
            value_low.reshape(token_count, head_width),
        ],
        axis=1,
    )
    qkv_weight_grad = jnp.dot(tokens.T, merged, preferred_element_type=jnp.float32)
    input_part = jnp.dot(merged, w_qkv.T, preferred_element_type=jnp.float32)
    input_sum = lax.psum(input_part.astype(jnp.bfloat16), "tensor").astype(jnp.float32)
    input_grad = grad_one + input_sum
    query_bias_grad = jnp.sum(merged[:, :head_width].astype(jnp.float32), axis=0)
    value_bias_grad = jnp.sum(merged[:, 2 * head_width :].astype(jnp.float32), axis=0)
    qkv_piece = jnp.concatenate(
        [
            qkv_weight_grad[:, part_index * head_width : part_index * head_width + piece_width]
            for part_index in range(3)
        ],
        axis=1,
    )
    block_list = [pack(qkv_piece, out_weight_grad, up_weight_grad, down_weight_grad, block_edge)]
    split_list = [jnp.concatenate([query_bias_grad, value_bias_grad, up_bias_grad])]
    padded = jnp.concatenate(
        [jnp.stack(block_list), jnp.zeros((piece_count, 1, block_edge, block_edge), jnp.float32)],
        axis=1,
    )
    split_local = jnp.stack(split_list)
    row_local = jnp.stack(
        [
            out_bias_grad,
            gain_one_grad,
            shift_one_grad,
            down_bias_grad,
            gain_two_grad,
            shift_two_grad,
        ]
    )
    token_total = tokens.shape[0] * lax.axis_size("dp")
    mean_scale = 1.0 / token_total
    slot_terms = jnp.take(padded[0], block_of_slot, axis=0)
    owned_sum = lax.psum_scatter(slot_terms[None], "dp", scatter_dimension=1, tiled=True)[0]
    split_total, row_total = lax.psum((split_local, row_local), "dp")
    weight_grads = (owned_sum * mean_scale)[None]
    split_grad = split_total * mean_scale
    row_grad = row_total * mean_scale
    new_masters, new_first, new_second = rotate_update(
        weight_grads, mom_first, mom_second, left_bases, right_bases, masters
    )
    new_split, new_split_first, new_split_second = adam_vector(
        split_grad, split_first, split_second, split_vec
    )
    new_row, new_row_first, new_row_second = adam_vector(row_grad, row_first, row_second, row_vec)
    return (
        layer_out,
        input_grad,
        weight_grads,
        new_masters,
        new_first,
        new_second,
        new_masters.astype(jnp.bfloat16),
        split_grad,
        new_split,
        new_split_first,
        new_split_second,
        row_grad,
        new_row,
        new_row_first,
        new_row_second,
    )


def solution(mesh):
    in_specs = (
        P("dp", None),
        P("dp", None),
        P("dp", None),
        P(),
        P("tensor", "dp", None, None),
        P("tensor", "dp", None, None),
        P("tensor", "dp", None, None),
        P("tensor", "dp", None, None),
        P("tensor", "dp", None, None),
        P("tensor", None),
        P("tensor", None),
        P("tensor", None),
        P(),
        P(),
        P(),
    )
    out_specs = (
        P("dp", None),
        P("dp", None),
        P("tensor", "dp", None, None),
        P("tensor", "dp", None, None),
        P("tensor", "dp", None, None),
        P("tensor", "dp", None, None),
        P("tensor", "dp", None, None),
        P("tensor", None),
        P("tensor", None),
        P("tensor", None),
        P("tensor", None),
        P(),
        P(),
        P(),
        P(),
    )
    return jax.shard_map(body, mesh=mesh, in_specs=in_specs, out_specs=out_specs, check_vma=False)
```

profile of v0, /device:TPU:0, one launch (start us, length us, event | category | flops | bytes accessed | tf_op | source)
XLA Modules:
  0.0 963.8 jit_solution(1679325248533685842)
XLA Ops:
  12.0 69.9 %all-gather.2.cloned.1.call-done = bf16[1,224,128,128]{3,2,0,1:T(8,128)(2,1)} async-done(((bf16[1,14,128,128]{3,2,0,1:T(8,128)(2,1)}), bf16[1,224,128,128]{3,2,0,1:T(8,128)(2,1)}) %all-gather.2.cloned.1.call-update) | async-done | bytes 7340048 | tf_op jit(solution)/shard_map/all_gather | solution.py:153
  81.9 11.4 %gather_fusion = bf16[216,128,128]{2,1,0:T(8,128)(2,1)} fusion(bf16[224,128,128]{2,1,0:T(8,128)(2,1)} %bitcast.275, s32[1024]{0:T(1024)S(1)} %pad_clamp_fusion.1), kind=kCustom, calls=%fused_computation | custom fusion | bytes 14156640 | tf_op jit(solution)/shard_map/jit(_take)/gather | solution.py:158
  102.6 6.5 convolution_bitcast_fusion
  130.7 32.0 %while.26 = (s32[]{:T(128)}, bf16[4,512,6,64]{1,3,2,0:T(8,128)(2,1)}, f32[4,6,512,1]{2,1,3,0:T(8,128)}, bf16[4,512,6,64]{1,3,2,0:T(8,128)(2,1)}, s32[4,512]{1,0:...) while((s32[]{:T(128)}, ...), condition=%wide.region_6.7_spmd, body=%wide.region_3.6_spmd.sunk | while | flops 420410368 | bytes 21607000 | solution.py:207
  181.6 74.1 %all-reduce.7.cloned.1.call-done = bf16[2048,768]{1,0:T(8,128)(2,1)} async-done(((bf16[2048,768]{1,0:T(8,128)(2,1)}), bf16[2048,768]{1,0:T(8,128)(2,1)}) %all-reduce.7.cloned.1.call-update) | async-done | bytes 3145744 | tf_op jit(solution)/shard_map/psum | solution.py:210
  262.9 35.6 %multiply_convert_fusion.1 = (bf16[2048,1536]{1,0:T(8,128)(2,1)S(1)}, f32[2048,1536]{1,0:T(8,128)}, f32[2048,1536]{1,0:T(8,128)}) fusion(f32[1536]{0:T(1024)S(1)} %slice_reduce_fusion, bf16[96,8,12,128]{3,2,1,0:T(8,128)(2,1)S(1)} %bitcast.285, f32[768]{0:T(1024)S(1)} %get-tuple-element.189, f32[768]{0:T(1024)S(1)} %get-tuple-element.190, ...), kind=kOutput, calls=%fused_computation.76 | convolution fusion | flops 5053612032 | bytes 40139776 | tf_op jit(solution)/shard_map/dot_general | solution.py:214
  301.2 6.4 convolution_convert_fusion.3
  307.6 85.9 %all-reduce.9.cloned.1.call-done = bf16[2048,768]{1,0:T(8,128)(2,1)} async-done(((bf16[2048,768]{1,0:T(8,128)(2,1)}), bf16[2048,768]{1,0:T(8,128)(2,1)}) %all-reduce.9.cloned.1.call-update) | async-done | bytes 3145744 | tf_op jit(solution)/shard_map/psum | solution.py:218
  393.5 5.6 fusion.122
  409.2 19.8 %convert_reduce_fusion = (f32[1536]{0:T(1024)}, bf16[2048,1536]{1,0:T(8,128)(2,1)}) fusion(f32[2048,1536]{1,0:T(8,128)} %get-tuple-element.248, bf16[192,8,6,128]{3,2,1,0:T(8,128)(2,1)} %bitcast.286, f32[2048,768]{1,0:T(8,128)} %get-tuple-element.244, f32[2048]{0:T(1024)S(1)} %negate_multiply_fusion.2, f32[2048,1536]{1,0:T(8,128)} %get-tuple-element.263, ...), kind=kOutput, calls=%fused_computation.74 | convolution fusion | flops 4888459776 | bytes 40128512 | tf_op jit(solution)/shard_map/dot_general | solution.py:226
  429.0 9.3 convolution_convert_fusion.2
  439.6 84.7 %all-reduce.11.cloned.1.call-done = bf16[2048,768]{1,0:T(8,128)(2,1)} async-done(((bf16[2048,768]{1,0:T(8,128)(2,1)}), bf16[2048,768]{1,0:T(8,128)(2,1)}) %all-reduce.11.cloned.1.call-update) | async-done | bytes 3145744 | tf_op jit(solution)/shard_map/psum | solution.py:231
  524.3 10.4 %multiply_reduce_fusion.1 = (f32[768]{0:T(1024)}, f32[2048]{0:T(1024)S(1)}, f32[768]{0:T(1024)}, f32[768]{0:T(1024)}) fusion(f32[2048]{0:T(1024)S(1)} %fusion.109, bf16[2048,768]{1,0:T(8,128)(2,1)} %all-reduce.11.cloned.1.call-done, f32[2048,768]{1,0:T(8,128)} %get-tuple-element.244, f32[2048]{0:T(1024)S(1)} %negate_multiply_fusion.2, ...), kind=kLoop, calls=%fused_computation.101 | loop fusion | flops 25161472 | bytes 15776768 | tf_op jit(solution)/shard_map/transpose(jvp())/reduce_sum | solution.py:25
  534.7 6.1 fusion.120
  557.5 71.9 %while.27 = (s32[]{:T(128)}, bf16[4,512,6,64]{1,3,2,0:T(8,128)(2,1)}, bf16[4,512,6,64]{1,3,2,0:T(8,128)(2,1)}, bf16[4,512,6,64]{1,3,2,0:T(8,128)(2,1)}, bf16[4,5...) while((s32[]{:T(128)}, ...), condition=%wide.region_20.21_spmd, body=%wide.region_18.20_spmd.sunk | while | flops 1031468032 | bytes 52264052 | solution.py:267
  638.7 5.9 convolution_convert_fusion
  644.7 12.5 %fusion.114 = f32[768,1536]{1,0:T(8,128)} fusion(bf16[2048,1536]{1,0:T(8,128)(2,1)} %get-tuple-element.267, f32[768]{0:T(1024)S(1)} %copy-done.44, f32[768]{0:T(1024)S(1)} %get-tuple-element.190, f32[2048]{0:T(1024)S(1)} %fusion.109, bf16[2048,768]{1,0:T(8,128)(2,1)} %all-reduce.7.cloned.1.call-done, bf16[2048,768]{1,0:T(8,128)(2,1)} %param.19, ...), kind=kOutput, calls=%fused_computation.216 | convolution fusion | flops 4845993984 | bytes 17327104 | tf_op jit(solution)/shard_map/dot_general | solution.py:229
  657.2 7.0 reshape.345
  664.1 6.5 copy.119
  670.6 9.0 fusion.112
  679.6 6.6 reshape.347
  686.2 6.0 copy.120
  692.3 5.7 convolution_bitcast_fusion.1
  702.8 5.5 copy.117
  708.2 22.3 %all-reduce.13.cloned.1.call-done = bf16[2048,768]{1,0:T(8,128)(2,1)} async-done(((bf16[2048,768]{1,0:T(8,128)(2,1)}), bf16[2048,768]{1,0:T(8,128)(2,1)}) %all-reduce.13.cloned.1.call-update) | async-done | bytes 3145744 | tf_op jit(solution)/shard_map/psum | solution.py:280
  730.6 6.5 add_reduce_fusion
  746.1 8.4 maximum_bitcast_fusion
  754.5 12.7 %pad_bitcast_fusion = f32[217,128,128]{2,1,0:T(8,128)} fusion(f32[1,216,128,128]{3,2,1,0:T(8,128)} %maximum_bitcast_fusion), kind=kLoop, calls=%fused_computation.71 | loop fusion | bytes 28377088 | tf_op jit(solution)/shard_map/squeeze | solution.py:310
  767.2 16.6 %gather_fusion.1 = f32[224,128,128]{2,1,0:T(8,128)} fusion(f32[217,128,128]{2,1,0:T(8,128)} %pad_bitcast_fusion, s32[1024]{0:T(1024)} %pad_clamp_fusion), kind=kCustom, calls=%fused_computation.1 | custom fusion | bytes 29361024 | tf_op jit(solution)/shard_map/jit(_take)/gather | solution.py:310
  783.8 11.4 %bitcast_select_fusion = f32[1,224,128,128]{3,2,1,0:T(8,128)} fusion(f32[224,128,128]{2,1,0:T(8,128)} %gather_fusion.1, pred[224]{0:T(512)(128)(4,1)S(1)} %copy-done.48), kind=kLoop, calls=%fused_computation.70 | loop fusion | flops 3670016 | bytes 29360352 | tf_op jit(solution)/shard_map/jit(_take)/select_n | solution.py:310
  799.6 63.2 %all-reduce.1 = (f32[1,2304]{1,0:T(1,128)S(1)}, f32[6,768]{1,0:T(8,128)S(1)}) all-reduce(f32[1,2304]{1,0:T(1,128)S(1)} %stack.20, f32[6,768]{1,0:T(8,128)S(1)} %stack.23), channel_id=1, replica_groups=mesh['dp'=16,'tensor'=2] {'dp'}, use_global_device_ids=true, to_apply=%region_26.27 | all-reduce | flops 6912 | bytes 55296 | tf_op jit(solution)/shard_map/psum | solution.py:312
  864.2 81.2 %reduce-scatter.2.cloned.1.call-done = f32[1,14,128,128]{3,2,1,0:T(8,128)} async-done(((f32[1,224,128,128]{3,2,1,0:T(8,128)}), f32[1,14,128,128]{3,2,1,0:T(8,128)}) %reduce-scatter.2.cloned.1.call-update) | async-done | bytes 917520 | tf_op jit(solution)/shard_map/reduce_scatter | solution.py:311
  (273 shorter events, 235.1 us)
Async XLA Ops:
  7.2 942.6 %copy-start = (f32[1,14,128,128]{3,2,1,0:T(8,128)S(1)}, f32[1,14,128,128]{3,2,1,0:T(8,128)}, u32[]{:S(2)}) copy-start(f32[1,14,128,128]{3,2,1,0:T(8,128)} %param.27) | copy-start | bytes 2752516
  7.2 74.7 %all-gather.2.cloned.1.call-start = ((), (), s32[]{:S(2)}) async-start(), calls=%async_computation.1 | async-start | bytes 7798784 | tf_op jit(solution)/shard_map/all_gather | solution.py:153
  9.4 246.3 %all-reduce.7.cloned.1.call-start = ((), (), s32[]{:S(2)}) async-start(), calls=%async_computation.2 | async-start | bytes 6291456 | tf_op jit(solution)/shard_map/psum | solution.py:210
  162.7 8.6 copy-start.6
  162.7 8.6 copy-start.29
  171.3 222.2 %all-reduce.9.cloned.1.call-start = ((), (), s32[]{:S(2)}) async-start(), calls=%async_computation.3 | async-start | bytes 6291456 | tf_op jit(solution)/shard_map/psum | solution.py:218
  171.5 222.0 %copy-start.43 = (f32[768]{0:T(1024)}, f32[768]{0:T(1024)S(1)}, u32[]{:S(2)}) copy-start(f32[768]{0:T(1024)S(1)} %get-tuple-element.189) | copy-start | bytes 9220
  255.7 7.2 copy-start.17
  262.9 38.3 %copy-start.18 = (bf16[12,6,128,128]{3,1,2,0:T(8,128)(2,1)S(1)}, bf16[12,6,128,128]{3,1,2,0:T(8,128)(2,1)}, u32[]{:S(2)}) copy-start(bf16[12,6,128,128]{3,1,2,0:T(8,128)(2,1)} %copy.108) | copy-start | bytes 7077892
  307.6 216.7 %all-reduce.11.cloned.1.call-start = ((), (), s32[]{:S(2)}) async-start(), calls=%async_computation.4 | async-start | bytes 6291456 | tf_op jit(solution)/shard_map/psum | solution.py:231
  429.0 9.4 copy-start.47
  438.3 292.2 %all-reduce.13.cloned.1.call-start = ((), (), s32[]{:S(2)}) async-start(), calls=%async_computation.5 | async-start | bytes 6291456 | tf_op jit(solution)/shard_map/psum | solution.py:280
  439.6 95.1 %copy-start.33 = (f32[2048]{0:T(1024)S(1)}, f32[2048]{0:T(1024)}, u32[]{:S(2)}) copy-start(f32[2048]{0:T(1024)} %copy-done.32) | copy-start | bytes 24580
  524.3 10.4 %copy-start.2 = (bf16[2048,768]{1,0:T(8,128)(2,1)S(1)}, bf16[2048,768]{1,0:T(8,128)(2,1)}, u32[]{:S(2)}) copy-start(bf16[2048,768]{1,0:T(8,128)(2,1)} %param.19) | copy-start | bytes 9437188
  524.3 10.4 %copy-start.5 = (bf16[2048,768]{1,0:T(8,128)(2,1)S(1)}, bf16[2048,768]{1,0:T(8,128)(2,1)}, u32[]{:S(2)}) copy-start(bf16[2048,768]{1,0:T(8,128)(2,1)} %all-reduce.7.cloned.1.call-done) | copy-start | bytes 9437188
  524.3 10.4 %copy-start.12 = (bf16[2048,768]{1,0:T(8,128)(2,1)S(1)}, bf16[2048,768]{1,0:T(8,128)(2,1)}, u32[]{:S(2)}) copy-start(bf16[2048,768]{1,0:T(8,128)(2,1)} %all-reduce.11.cloned.1.call-done) | copy-start | bytes 9437188
  534.7 8.8 copy-start.27
  644.6 300.8 %reduce-scatter.2.cloned.1.call-start = ((), (), s32[]{:S(2)}) async-start(), calls=%async_computation.6 | async-start | bytes 15597568 | tf_op jit(solution)/shard_map/reduce_scatter | solution.py:311
  657.2 13.5 %slice-start = ((s8[6291456]{0:T(1024)(128)(4,1)}), s8[2097152]{0:T(1024)(128)(4,1)S(1)}, s32[]{:S(2)}) async-start(s8[6291456]{0:T(1024)(128)(4,1)} %bitcast.262), calls=%async_computation.7 | async-start | bytes 4194304
  679.6 12.7 %slice-start.4 = ((s8[4718592]{0:T(1024)(128)(4,1)}), s8[524288]{0:T(1024)(128)(4,1)S(1)}, s32[]{:S(2)}) async-start(s8[4718592]{0:T(1024)(128)(4,1)} %bitcast.296), calls=%async_computation.11 | async-start | bytes 1048576
  737.1 8.3 slice-start.2
  767.2 16.6 %copy-start.48 = (pred[224]{0:T(512)(128)(4,1)S(1)}, pred[224]{0:T(512)(128)(4,1)}, u32[]{:S(2)}) copy-start(pred[224]{0:T(512)(128)(4,1)} %compare_and_fusion) | copy-start | bytes 676
  795.3 67.6 %copy-start.31 = (f32[6,768]{1,0:T(8,128)S(1)}, f32[6,768]{1,0:T(8,128)}, u32[]{:S(2)}) copy-start(f32[6,768]{1,0:T(8,128)} %param.31) | copy-start | bytes 55300
  795.3 67.6 %copy-start.36 = (f32[6,768]{1,0:T(8,128)S(1)}, f32[6,768]{1,0:T(8,128)}, u32[]{:S(2)}) copy-start(f32[6,768]{1,0:T(8,128)} %param.32) | copy-start | bytes 55300
  795.3 67.6 %copy-start.37 = (f32[6,768]{1,0:T(8,128)S(1)}, f32[6,768]{1,0:T(8,128)}, u32[]{:S(2)}) copy-start(f32[6,768]{1,0:T(8,128)} %param.33) | copy-start | bytes 55300
  795.3 68.2 %copy-start.35 = (f32[1,2304]{1,0:T(1,128)S(1)}, f32[1,2304]{1,0:T(1,128)}, u32[]{:S(2)}) copy-start(f32[1,2304]{1,0:T(1,128)} %param.28) | copy-start | bytes 27652
  795.3 68.2 %copy-start.45 = (f32[1,2304]{1,0:T(1,128)S(1)}, f32[1,2304]{1,0:T(1,128)}, u32[]{:S(2)}) copy-start(f32[1,2304]{1,0:T(1,128)} %param.29) | copy-start | bytes 27652
  795.3 68.2 %copy-start.46 = (f32[1,2304]{1,0:T(1,128)S(1)}, f32[1,2304]{1,0:T(1,128)}, u32[]{:S(2)}) copy-start(f32[1,2304]{1,0:T(1,128)} %param.30) | copy-start | bytes 27652
  795.4 154.5 %copy-start.22 = (f32[1,14,128,128]{3,2,1,0:T(8,128)S(1)}, f32[1,14,128,128]{3,2,1,0:T(8,128)}, u32[]{:S(2)}) copy-start(f32[1,14,128,128]{3,2,1,0:T(8,128)} %param.25) | copy-start | bytes 2752516
  798.6 153.7 %copy-start.23 = (f32[1,14,128,128]{3,2,1,0:T(8,128)S(1)}, f32[1,14,128,128]{3,2,1,0:T(8,128)}, u32[]{:S(2)}) copy-start(f32[1,14,128,128]{3,2,1,0:T(8,128)} %param.26) | copy-start | bytes 2752516
  946.6 10.1 %copy-start.15 = (f32[1,14,128,128]{3,2,1,0:T(8,128)}, f32[1,14,128,128]{3,2,1,0:T(8,128)S(1)}, u32[]{:S(2)}) copy-start(f32[1,14,128,128]{3,2,1,0:T(8,128)S(1)} %broadcast_multiply_fusion) | copy-start | bytes 2752516
  946.6 7.0 copy-start.16
  (30 other events, 92.2 us)
Sparse Core Ops, SparseCore 0:
  10.9 70.9 all-gather.1
  171.4 84.1 all-reduce.6
  307.7 85.7 all-reduce.8
  438.4 85.7 all-reduce.10
  644.7 85.7 all-reduce.12
  795.5 149.8 reduce-scatter.1
where the time goes:
time: 974 us; the launch traced here: 964 us
  waiting for transfers between devices  418 us (43%)
  matrix products  210 us (22%)
  local copies, waits for them, and re-layouts  159 us (16%)
  other arithmetic  96.8 us (10%)
  blocking collectives  63.2 us (6%)
  between operations  15.1 us (2%)
    psum x1, waiting for transfers between devices, body(): lax.psum(down_part.astype(jnp.bfloat16), 'tensor').astype(jnp.float32)  85.9 us
    psum x1, waiting for transfers between devices, body(): lax.psum(back_part.astype(jnp.bfloat16), 'tensor').astype(jnp.float32)  84.7 us
    reduce_scatter x1, waiting for transfers between devices, body(): lax.psum_scatter(slot_terms[None], 'dp', scatter_dimension=1, tiled=True)[0]  81.2 us
    psum x1, waiting for transfers between devices, body(): lax.psum(attn_part.astype(jnp.bfloat16), 'tensor').astype(jnp.float32)  74.1 us
    all_gather x1, waiting for transfers between devices, body(): lax.all_gather(masters.astype(jnp.bfloat16), 'dp', axis=1, tiled=True)  69.9 us
    psum x1, blocking collectives, body(): split_total, row_total = lax.psum((split_local, row_local), 'dp')  63.2 us
    dot_general x1, matrix products, body(): jnp.dot(normed_low, w_up, preferred_element_type=jnp.float32) + up_bias  35.6 us
    psum x1, waiting for transfers between devices, body(): lax.psum(input_part.astype(jnp.bfloat16), 'tensor').astype(jnp.float32)  22.3 us
  transfers between devices with their start and end apart: 6, of which 6 were waited for; matrix products, arithmetic and copies ran while one was open for 8% of the time, Pallas kernels for 0%

commit v1 on v0

--- a/solution.py
+++ b/solution.py
@@ -144,51 +144,53 @@
     row_second,
 ):
     pieces = lax.axis_size("tensor")
+    piece = lax.axis_index("tensor")
     piece_width = HEADS * HEAD // pieces
     piece_ffn = FF // pieces
     block_edge = masters.shape[-1]
-    counts_list = block_counts(block_edge, piece_width, piece_ffn)
-    block_total = counts_list[0] + counts_list[1] + counts_list[2] + counts_list[3]
+    block_total = sum(block_counts(block_edge, piece_width, piece_ffn))
+    slots = block_of_slot.shape[0]
     full_seq = tokens.shape[0] // pair_lengths.shape[0]
-    everyone = lax.all_gather(masters.astype(jnp.bfloat16), "dp", axis=1, tiled=True)
+    row_count = pair_lengths.shape[0] // pieces
+    token_count = row_count * full_seq
+    tokens_own = lax.dynamic_slice_in_dim(tokens, piece * token_count, token_count, 0)
+    cotangent_own = lax.dynamic_slice_in_dim(cotangent, piece * token_count, token_count, 0)
+    pairs_own = lax.dynamic_slice_in_dim(pair_lengths, piece * row_count, row_count, 0)
+    everyone = lax.all_gather(
+        masters[0].astype(jnp.bfloat16), ("tensor", "dp"), axis=0, tiled=True
+    ).reshape(pieces, slots, block_edge, block_edge)
     slot_of = slot_table(block_of_slot, block_total)
-    local_heads = HEADS // pieces
-    piece_count = everyone.shape[0]
-    head_width = local_heads * HEAD
-    unpacked = [unpack(jnp.take(everyone[0], slot_of, axis=0), block_edge, piece_width, piece_ffn)]
+    unpacked = [
+        unpack(jnp.take(everyone[index], slot_of, axis=0), block_edge, piece_width, piece_ffn)
+        for index in range(pieces)
+    ]
     w_qkv = jnp.concatenate(
         [
-            jnp.concatenate(
-                [
-                    one_piece[0][:, part_index * piece_width : (part_index + 1) * piece_width]
-                    for one_piece in unpacked
-                ],
-                axis=1,
-            )
+            one_piece[0][:, part_index * piece_width : (part_index + 1) * piece_width]
             for part_index in range(3)
+            for one_piece in unpacked
         ],
         axis=1,
     )
     w_out = jnp.concatenate([one_piece[1] for one_piece in unpacked], axis=0)
     w_up = jnp.concatenate([one_piece[2] for one_piece in unpacked], axis=1)
     w_down = jnp.concatenate([one_piece[3] for one_piece in unpacked], axis=0)
-    query_bias = split_vec[0][:piece_width]
-    value_bias = split_vec[0][piece_width : 2 * piece_width]
-    up_bias = split_vec[0][2 * piece_width :]
+    split_all = lax.all_gather(split_vec[0], "tensor", axis=0)
+    query_bias = split_all[:, :piece_width].reshape(-1)
+    value_bias = split_all[:, piece_width : 2 * piece_width].reshape(-1)
+    up_bias = split_all[:, 2 * piece_width :].reshape(-1)
     out_bias, gain_one, shift_one, down_bias, gain_two, shift_two = (
         row_vec[row_number] for row_number in range(6)
     )
-    token_count = tokens.shape[0]
-    row_count = pair_lengths.shape[0]
-    seg_rows = segment_ids(pair_lengths, full_seq)
-    inputs = tokens.astype(jnp.float32)
-    projected = jnp.dot(tokens, w_qkv, preferred_element_type=jnp.float32)
-    queries = (projected[:, :head_width] + query_bias).astype(jnp.bfloat16)
-    keys_proj = projected[:, head_width : 2 * head_width].astype(jnp.bfloat16)
-    values = (projected[:, 2 * head_width :] + value_bias).astype(jnp.bfloat16)
-    query_rows = split_heads(queries, row_count, full_seq, local_heads)
-    key_rows = split_heads(keys_proj, row_count, full_seq, local_heads)
-    value_rows = split_heads(values, row_count, full_seq, local_heads)
+    seg_rows = segment_ids(pairs_own, full_seq)
+    inputs = tokens_own.astype(jnp.float32)
+    projected = jnp.dot(tokens_own, w_qkv, preferred_element_type=jnp.float32)
+    queries = (projected[:, :D] + query_bias).astype(jnp.bfloat16)
+    keys_proj = projected[:, D : 2 * D].astype(jnp.bfloat16)
+    values = (projected[:, 2 * D :] + value_bias).astype(jnp.bfloat16)
+    query_rows = split_heads(queries, row_count, full_seq, HEADS)
+    key_rows = split_heads(keys_proj, row_count, full_seq, HEADS)
+    value_rows = split_heads(values, row_count, full_seq, HEADS)
 
     def forward_row(row_items):
         query_row, key_row, value_row, seg_row = row_items
@@ -205,21 +207,20 @@
         return (mixed.astype(jnp.bfloat16), log_total)
 
     mapped = lax.map(forward_row, (query_rows, key_rows, value_rows, seg_rows))
-    attended = mapped[0].reshape(token_count, head_width)
-    attn_part = jnp.dot(attended, w_out, preferred_element_type=jnp.float32)
-    attn_sum = lax.psum(attn_part.astype(jnp.bfloat16), "tensor").astype(jnp.float32)
+    attended = mapped[0].reshape(token_count, D)
+    attn_sum = jnp.dot(attended, w_out, preferred_element_type=jnp.float32)
     hidden_one = inputs + attn_sum + out_bias
     normed_one, norm_one_back = jax.vjp(norm_row, hidden_one, gain_one, shift_one)
     normed_low = normed_one.astype(jnp.bfloat16)
     up_pre = jnp.dot(normed_low, w_up, preferred_element_type=jnp.float32) + up_bias
     active, gelu_back = jax.vjp(gelu_exact, up_pre)
     active_low = active.astype(jnp.bfloat16)
-    down_part = jnp.dot(active_low, w_down, preferred_element_type=jnp.float32)
-    down_sum = lax.psum(down_part.astype(jnp.bfloat16), "tensor").astype(jnp.float32)
+    down_sum = jnp.dot(active_low, w_down, preferred_element_type=jnp.float32)
     hidden_two = normed_one + down_sum + down_bias
     output, norm_two_back = jax.vjp(norm_row, hidden_two, gain_two, shift_two)
-    layer_out = output.astype(jnp.bfloat16)
-    grad_two, gain_two_grad, shift_two_grad = norm_two_back(cotangent.astype(jnp.float32))
+    layer_own = output.astype(jnp.bfloat16)
+    layer_out = lax.all_gather(layer_own, "tensor", axis=0, tiled=True)
+    grad_two, gain_two_grad, shift_two_grad = norm_two_back(cotangent_own.astype(jnp.float32))
     down_low = grad_two.astype(jnp.bfloat16)
     down_bias_grad = jnp.sum(grad_two, axis=0)
     down_weight_grad = jnp.dot(active_low.T, down_low, preferred_element_type=jnp.float32)
@@ -227,15 +228,14 @@
     up_low = gelu_back(grad_active)[0].astype(jnp.bfloat16)
     up_bias_grad = jnp.sum(up_low.astype(jnp.float32), axis=0)
     up_weight_grad = jnp.dot(normed_low.T, up_low, preferred_element_type=jnp.float32)
-    back_part = jnp.dot(up_low, w_up.T, preferred_element_type=jnp.float32)
-    back_sum = lax.psum(back_part.astype(jnp.bfloat16), "tensor").astype(jnp.float32)
+    back_sum = jnp.dot(up_low, w_up.T, preferred_element_type=jnp.float32)
     grad_normed = grad_two + back_sum
     grad_one, gain_one_grad, shift_one_grad = norm_one_back(grad_normed)
     out_bias_grad = jnp.sum(grad_one, axis=0)
     attn_low = grad_one.astype(jnp.bfloat16)
     out_weight_grad = jnp.dot(attended.T, attn_low, preferred_element_type=jnp.float32)
     mixed_low = jnp.dot(attn_low, w_out.T, preferred_element_type=jnp.float32).astype(jnp.bfloat16)
-    grad_rows = split_heads(mixed_low, row_count, full_seq, local_heads)
+    grad_rows = split_heads(mixed_low, row_count, full_seq, HEADS)
 
     def backward_row(row_items):
         query_row, key_row, value_row, seg_row, grad_row, log_total = row_items
@@ -263,35 +263,52 @@
             value_grad.astype(jnp.bfloat16),
         )
 
-    saved_rows = mapped[1]
     query_low, key_low, value_low = lax.map(
-        backward_row, (query_rows, key_rows, value_rows, seg_rows, grad_rows, saved_rows)
+        backward_row, (query_rows, key_rows, value_rows, seg_rows, grad_rows, mapped[1])
     )
     merged = jnp.concatenate(
         [
-            query_low.reshape(token_count, head_width),
-            key_low.reshape(token_count, head_width),
-            value_low.reshape(token_count, head_width),
+            query_low.reshape(token_count, D),
+            key_low.reshape(token_count, D),
+            value_low.reshape(token_count, D),
         ],
         axis=1,
     )
-    qkv_weight_grad = jnp.dot(tokens.T, merged, preferred_element_type=jnp.float32)
-    input_part = jnp.dot(merged, w_qkv.T, preferred_element_type=jnp.float32)
-    input_sum = lax.psum(input_part.astype(jnp.bfloat16), "tensor").astype(jnp.float32)
-    input_grad = grad_one + input_sum
-    query_bias_grad = jnp.sum(merged[:, :head_width].astype(jnp.float32), axis=0)
-    value_bias_grad = jnp.sum(merged[:, 2 * head_width :].astype(jnp.float32), axis=0)
-    qkv_piece = jnp.concatenate(
-        [
-            qkv_weight_grad[:, part_index * head_width : part_index * head_width + piece_width]
-            for part_index in range(3)
+    qkv_weight_grad = jnp.dot(tokens_own.T, merged, preferred_element_type=jnp.float32)
+    input_own = grad_one + jnp.dot(merged, w_qkv.T, preferred_element_type=jnp.float32)
+    input_grad = lax.all_gather(
+        input_own.astype(jnp.bfloat16), "tensor", axis=0, tiled=True
+    ).astype(jnp.float32)
+    query_bias_grad = jnp.sum(merged[:, :D].astype(jnp.float32), axis=0)
+    value_bias_grad = jnp.sum(merged[:, 2 * D :].astype(jnp.float32), axis=0)
+    block_list = []
+    split_list = []
+    for index in range(pieces):
+        heads_at = slice(index * piece_width, (index + 1) * piece_width)
+        ffn_at = slice(index * piece_ffn, (index + 1) * piece_ffn)
+        qkv_piece = jnp.concatenate(
+            [qkv_weight_grad[:, part * D : (part + 1) * D][:, heads_at] for part in range(3)],
+            axis=1,
+        )
+        block_list.append(
+            pack(
+                qkv_piece,
+                out_weight_grad[heads_at],
+                up_weight_grad[:, ffn_at],
+                down_weight_grad[ffn_at],
+                block_edge,
+            )
+        )
+        split_list.append(
+            jnp.concatenate(
+                [query_bias_grad[heads_at], value_bias_grad[heads_at], up_bias_grad[ffn_at]]
+            )
+        )
+    padded = jnp.concatenate(
+        [
+            jnp.stack(block_list).astype(jnp.bfloat16),
+            jnp.zeros((pieces, 1, block_edge, block_edge), jnp.bfloat16),
         ],
-        axis=1,
-    )
-    block_list = [pack(qkv_piece, out_weight_grad, up_weight_grad, down_weight_grad, block_edge)]
-    split_list = [jnp.concatenate([query_bias_grad, value_bias_grad, up_bias_grad])]
-    padded = jnp.concatenate(
-        [jnp.stack(block_list), jnp.zeros((piece_count, 1, block_edge, block_edge), jnp.float32)],
         axis=1,
     )
     split_local = jnp.stack(split_list)
@@ -307,11 +324,16 @@
     )
     token_total = tokens.shape[0] * lax.axis_size("dp")
     mean_scale = 1.0 / token_total
-    slot_terms = jnp.take(padded[0], block_of_slot, axis=0)
-    owned_sum = lax.psum_scatter(slot_terms[None], "dp", scatter_dimension=1, tiled=True)[0]
-    split_total, row_total = lax.psum((split_local, row_local), "dp")
+    slot_terms = jnp.take(padded, block_of_slot, axis=1)
+    owned_sum = lax.psum_scatter(
+        slot_terms.reshape(pieces * slots, block_edge, block_edge),
+        ("tensor", "dp"),
+        scatter_dimension=0,
+        tiled=True,
+    ).astype(jnp.float32)
+    split_total, row_total = lax.psum((split_local, row_local), ("tensor", "dp"))
     weight_grads = (owned_sum * mean_scale)[None]
-    split_grad = split_total * mean_scale
+    split_grad = lax.dynamic_slice_in_dim(split_total, piece, 1, 0) * mean_scale
     row_grad = row_total * mean_scale
     new_masters, new_first, new_second = rotate_update(
         weight_grads, mom_first, mom_second, left_bases, right_bases, masters

time: 974 us -> 786 us (0.81)
  waiting for transfers between devices: 418 us -> 194 us
  local copies, waits for them, and re-layouts: 159 us -> 273 us
  matrix products: 210 us -> 170 us
  other arithmetic: 96.8 us -> 70.8 us
  blocking collectives: 63.2 us -> 53 us
    psum x4 -> x0, waiting for transfers between devices: 267 us -> none  [the longest x1 85.9 us: body(): lax.psum(down_part.astype(jnp.bfloat16), 'tensor').astype(jnp.float32)]
    slice x3 -> x16, local copies, waits for them, and re-layouts: 2.15 us -> 33.3 us  [the longest x2 14.9 us: body(): keys_proj = projected[:, D:2 * D].astype(jnp.bfloat16)]
    unnamed x118 -> x179, local copies, waits for them, and re-layouts: 17.7 us -> 40.7 us
    all_gather x1 -> x3, waiting for transfers between devices: 69.9 us -> 92.7 us  [the longest x1 92.7 us: body(): lax.all_gather(masters[0].astype(jnp.bfloat16), ('tensor', 'dp'), axis=0,...]
    reduce_scatter x1, waiting for transfers between devices: 81.2 us -> 101 us  [body(): lax.psum_scatter(slot_terms.reshape(pieces * slots, block_edge, block_edg...]
    reshape x3 -> x8, local copies, waits for them, and re-layouts: 18.4 us -> 35.8 us  [to_blocks(): matrix.reshape(row_total // block_edge, block_edge, col_total // block_ed...]
    gather x2 -> x4, local copies, waits for them, and re-layouts: 28 us -> 44.5 us  [the longest x2 22.7 us: body(): jnp.take(everyone[index], slot_of, axis=0)]
    psum x1, blocking collectives: 63.2 us -> 47.5 us  [body(): lax.psum((split_local, row_local), ('tensor', 'dp'))]
  transfers between devices with their start and end apart: 6 -> 4, of which waited for: 6 -> 2; matrix products, arithmetic and copies ran while one was open for 8% -> 30% of each run, Pallas kernels for 0% -> 0%
where the time goes in v1:
time: 786 us; the launch traced here: 776 us
  local copies, waits for them, and re-layouts  273 us (35%)
  waiting for transfers between devices  194 us (25%)
  matrix products  170 us (22%)
  other arithmetic  70.8 us (9%)
  blocking collectives  53 us (7%)
  between operations  15.6 us (2%)
    reduce_scatter x1, waiting for transfers between devices, body(): lax.psum_scatter(slot_terms.reshape(pieces * slots, block_edge, block_edg...  101 us
    all_gather x1, waiting for transfers between devices, body(): lax.all_gather(masters[0].astype(jnp.bfloat16), ('tensor', 'dp'), axis=0,...  92.7 us
    psum x1, blocking collectives, body(): lax.psum((split_local, row_local), ('tensor', 'dp'))  47.5 us
    unnamed x179, local copies, waits for them, and re-layouts  40.7 us
    dot_general x1, matrix products, body(): jnp.dot(normed_low, w_up, preferred_element_type=jnp.float32) + up_bias  37.4 us
    reshape x8, local copies, waits for them, and re-layouts, to_blocks(): matrix.reshape(row_total // block_edge, block_edge, col_total // block_ed...  35.8 us
    transpose x8, local copies, waits for them, and re-layouts, to_blocks(): return shaped.transpose(0, 2, 1, 3).reshape(-1, block_edge, block_edge)  26.1 us
    gather x2, local copies, waits for them, and re-layouts, body(): jnp.take(everyone[index], slot_of, axis=0)  22.7 us
  transfers between devices with their start and end apart: 4, of which 2 were waited for; matrix products, arithmetic and copies ran while one was open for 30% of the time, Pallas kernels for 0%

profile of v1, /device:TPU:0, one launch (start us, length us, event | category | flops | bytes accessed | tf_op | source)
XLA Modules:
  0.0 776.2 jit_solution(18424600262570276187)
XLA Ops:
  11.7 5.5 all-gather.1
  26.9 92.7 %all-gather.10.cloned.1.call-done = bf16[1,448,128,128]{3,2,0,1:T(8,128)(2,1)} async-done(((bf16[1,14,128,128]{3,2,0,1:T(8,128)(2,1)}), bf16[1,448,128,128]{3,2,0,1:T(8,128)(2,1)}) %all-gather.10.cloned.1.call-update) | async-done | bytes 14680080 | tf_op jit(solution)/shard_map/all_gather | solution.py:159
  119.5 10.7 %slice_bitcast_fusion = (bf16[224,128,128]{2,1,0:T(8,128)(2,1)}, bf16[224,128,128]{2,1,0:T(8,128)(2,1)}) fusion(bf16[1,448,128,128]{3,2,0,1:T(8,128)(2,1)} %all-gather.10.cloned.1.call-done), kind=kLoop, calls=%fused_computation.91 | loop fusion | bytes 29360128 | tf_op jit(solution)/shard_map/slice | solution.py:164
  130.2 11.3 %gather_fusion.2 = bf16[216,128,128]{2,1,0:T(8,128)(2,1)} fusion(bf16[224,128,128]{2,1,0:T(8,128)(2,1)} %get-tuple-element.341, s32[1024]{0:T(1024)S(1)} %pad_clamp_fusion.1), kind=kCustom, calls=%fused_computation.1.clone | custom fusion | bytes 14156640 | tf_op jit(solution)/shard_map/jit(_take)/gather | solution.py:164
  141.6 11.4 %gather_fusion.1 = bf16[216,128,128]{2,1,0:T(8,128)(2,1)} fusion(bf16[224,128,128]{2,1,0:T(8,128)(2,1)} %get-tuple-element.342, s32[1024]{0:T(1024)S(1)} %pad_clamp_fusion.1), kind=kCustom, calls=%fused_computation.clone | custom fusion | bytes 14156640 | tf_op jit(solution)/shard_map/jit(_take)/gather | solution.py:164
  153.0 6.2 broadcast_select_fusion
  202.0 12.3 %slice.300 = bf16[1024,768]{1,0:T(8,128)(2,1)} slice(f32[1024,2304]{1,0:T(8,128)S(1)} %fusion.116), slice={[0:1024], [768:1536]} | slice | bytes 3145728 | tf_op jit(solution)/shard_map/slice | solution.py:189
  242.3 22.3 %while.26 = (s32[]{:T(128)}, bf16[2,512,12,64]{1,3,2,0:T(8,128)(2,1)}, f32[2,12,512,1]{2,1,3,0:T(8,128)S(1)}, bf16[2,512,12,64]{1,3,2,0:T(8,128)(2,1)}, s32[2,51...) while((s32[]{:T(128)}, ...), condition=%wide.region_6.8_spmd, body=%wide.region_3.7_spmd.sunk | while | flops 840558592 | bytes 42180708 | solution.py:209
  276.7 37.4 %multiply_convert_fusion.3 = (bf16[1024,3072]{1,0:T(8,128)(2,1)S(1)}, f32[1024,3072]{1,0:T(8,128)}, f32[1024,3072]{1,0:T(8,128)}) fusion(f32[3072]{0:T(1024)S(1)} %add.210, bf16[768,3072]{1,0:T(8,128)(2,1)S(1)} %bitcast_dynamic-update-slice_fusion.3, f32[1024,768]{0,1:T(8,128)S(1)} %get-tuple-element.375, f32[768]{0:T(1024)S(1)} %get-tuple-element.281, ...), kind=kOutput, calls=%fused_computation.77 | convolution fusion | flops 5043388416 | bytes 39348224 | tf_op jit(solution)/shard_map/dot_general | solution.py:215
  314.2 5.9 fusion.114
  326.1 7.0 convolution_convert_fusion
  333.2 17.7 %convert_reduce_fusion = (f32[3072]{0:T(1024)}, bf16[1024,3072]{1,0:T(8,128)(2,1)}) fusion(f32[1024,3072]{1,0:T(8,128)} %get-tuple-element.336, bf16[3072,768]{1,0:T(8,128)(2,1)} %copy-done.39, f32[1024,768]{0,1:T(8,128)S(1)} %get-tuple-element.334, f32[1024]{0:T(1024)S(1)} %negate_multiply_fusion.2, f32[1024,3072]{1,0:T(8,128)} %get-tuple-element.376, ...), kind=kOutput, calls=%fused_computation.75 | convolution fusion | flops 4886885376 | bytes 39350272 | tf_op jit(solution)/shard_map/dot_general | solution.py:227
  350.9 10.9 %multiply_reduce_fusion.1 = (f32[768]{0:T(1024)}, f32[1024]{0:T(1024)S(1)}, f32[768]{0:T(1024)}, f32[1024,768]{0,1:T(8,128)S(1)}) fusion(f32[1024,768]{0,1:T(8,128)} %copy-done.14, f32[1024]{0:T(1024)S(1)} %fusion.93, f32[1024]{0:T(1024)S(1)} %broadcast_multiply_fusion.3, f32[768]{0:T(1024)S(1)} %get-tuple-element.282, ...), kind=kOutput, calls=%fused_computation.114 | convolution fusion | flops 4839699456 | bytes 20472832 | tf_op jit(solution)/shard_map/dot_general | solution.py:231
  361.8 5.6 convolution_convert_fusion.1
  391.2 51.4 %while.27 = (s32[]{:T(128)}, bf16[2,512,12,64]{1,3,2,0:T(8,128)(2,1)}, bf16[2,512,12,64]{1,3,2,0:T(8,128)(2,1)}, bf16[2,512,12,64]{1,3,2,0:T(8,128)(2,1)}, bf16[...) while((s32[]{:T(128)}, ...), condition=%wide.region_17.19_spmd, body=%wide.region_15.18_spmd.sunk | while | flops 2062673920 | bytes 147524944 | solution.py:266
  398.5 6.8 multiply_reduce_fusion.6
  405.3 7.1 multiply_convert_fusion.5
  424.1 6.8 multiply_reduce_fusion.6
  431.0 7.1 multiply_convert_fusion.5
  458.0 6.0 reshape.407
  467.9 5.4 reshape.405
  482.6 6.8 convolution_convert_fusion.2
  520.1 6.0 reshape.415
  530.0 5.6 reshape.413
  539.8 8.6 %add_convert_fusion.1 = bf16[1024,768]{0,1:T(8,128)(2,1)} fusion(f32[1024,768]{0,1:T(8,128)S(1)} %copy-done.12, bf16[1024,2304]{0,1:T(8,128)(2,1)} %constant_dynamic-update-slice_fusion, bf16[768,2304]{0,1:T(8,128)(2,1)} %copy-done.52, f32[1024]{0:T(1024)S(1)} %copy-done.67), kind=kOutput, calls=%fused_computation.117 | convolution fusion | flops 3626237952 | bytes 12980224 | tf_op jit(solution)/shard_map/dot_general | solution.py:278
  555.0 8.2 %fusion.59 = bf16[2,217,128,128]{3,2,1,0:T(8,128)(2,1)} fusion(bf16[1,216,128,128]{3,2,1,0:T(8,128)(2,1)S(1)} %maximum_bitcast_fusion.1, bf16[1,216,128,128]{3,2,1,0:T(8,128)(2,1)S(1)} %maximum_bitcast_fusion), kind=kLoop, calls=%fused_computation.73 | loop fusion | flops 49774592 | bytes 28377088 | tf_op jit(solution)/shard_map/stack | solution.py:309
  563.1 14.4 %gather_fusion = bf16[224,2,128,128]{3,2,1,0:T(8,128)(2,1)} fusion(bf16[2,217,128,128]{3,2,1,0:T(8,128)(2,1)} %fusion.59, s32[1024]{0:T(1024)} %pad_clamp_fusion), kind=kCustom, calls=%fused_computation.2 | custom fusion | bytes 29361024 | tf_op jit(solution)/shard_map/jit(_take)/gather | solution.py:327
  577.5 7.4 copy.230
  584.9 6.9 bitcast_select_fusion
  597.9 47.5 %all-reduce.1 = (f32[2,2304]{1,0:T(2,128)S(1)}, f32[6,768]{1,0:T(8,128)S(1)}) all-reduce(f32[2,2304]{1,0:T(2,128)S(1)} %pad_maximum_fusion.2, f32[6,768]{1,0:T(8,128)S(1)} %stack.42), channel_id=1, replica_groups=mesh['dp'=16,'tensor'=2] {'tensor','dp'}, use_global_device_ids=true, to_apply=%region_22.24 | all-reduce | flops 9216 | bytes 73728 | tf_op jit(solution)/shard_map/psum | solution.py:334
  651.4 5.5 copy.236
  656.9 101.2 %reduce-scatter.2.cloned.1.call-done = bf16[14,128,128]{2,1,0:T(8,128)(2,1)} async-done(((bf16[448,128,128]{2,1,0:T(8,128)(2,1)}), bf16[14,128,128]{2,1,0:T(8,128)(2,1)}) %reduce-scatter.2.cloned.1.call-update) | async-done | bytes 458768 | tf_op jit(solution)/shard_map/reduce_scatter | solution.py:328
  (376 shorter events, 268.1 us)
Async XLA Ops:
  7.2 753.6 %copy-start = (f32[1,14,128,128]{3,2,1,0:T(8,128)S(1)}, f32[1,14,128,128]{3,2,1,0:T(8,128)}, u32[]{:S(2)}) copy-start(f32[1,14,128,128]{3,2,1,0:T(8,128)} %param.29) | copy-start | bytes 2752516
  7.2 112.3 %all-gather.10.cloned.1.call-start = ((), (), s32[]{:S(2)}) async-start(), calls=%async_computation.4 | async-start | bytes 15138816 | tf_op jit(solution)/shard_map/all_gather | solution.py:159
  9.4 637.4 %all-gather.6.cloned.1.call-start = ((), (), s32[]{:S(2)}) async-start(), calls=%async_computation.1 | async-start | bytes 4718592 | tf_op jit(solution)/shard_map/all_gather | solution.py:222
  20.5 5.7 copy-start.53
  264.7 5.3 copy-start.35
  268.4 7.4 slice-start.4
  270.0 5.8 slice-start.5
  271.7 42.5 %copy-start.14 = (f32[1024,768]{0,1:T(8,128)}, f32[1024,768]{0,1:T(8,128)S(1)}, u32[]{:S(2)}) copy-start(f32[1024,768]{0,1:T(8,128)S(1)} %get-tuple-element.375) | copy-start | bytes 9437188
  275.7 38.4 %copy-start.38 = (bf16[768,3072]{1,0:T(8,128)(2,1)}, bf16[768,3072]{1,0:T(8,128)(2,1)S(1)}, u32[]{:S(2)}) copy-start(bf16[768,3072]{1,0:T(8,128)(2,1)S(1)} %bitcast_dynamic-update-slice_fusion.3) | copy-start | bytes 14155780
  276.7 37.5 %copy-start.39 = (bf16[3072,768]{1,0:T(8,128)(2,1)}, bf16[3072,768]{1,0:T(8,128)(2,1)S(1)}, u32[]{:S(2)}) copy-start(bf16[3072,768]{1,0:T(8,128)(2,1)S(1)} %bitcast_dynamic-update-slice_fusion.1) | copy-start | bytes 14155780
  276.7 37.5 %copy-start.74 = (f32[768]{0:T(1024)S(1)}, f32[768]{0:T(1024)}, u32[]{:S(2)}) copy-start(f32[768]{0:T(1024)} %get-tuple-element.280) | copy-start | bytes 9220
  314.2 5.9 copy-start.77
  326.1 24.8 %copy-start.10 = (f32[1024,768]{0,1:T(8,128)}, f32[1024,768]{0,1:T(8,128)S(1)}, u32[]{:S(2)}) copy-start(f32[1024,768]{0,1:T(8,128)S(1)} %get-tuple-element.334) | copy-start | bytes 9437188
  326.1 24.8 %copy-start.64 = (f32[1024]{0:T(1024)}, f32[1024]{0:T(1024)S(1)}, u32[]{:S(2)}) copy-start(f32[1024]{0:T(1024)S(1)} %negate_multiply_fusion.2) | copy-start | bytes 12292
  350.9 10.9 %copy-start.15 = (f32[1024,768]{0,1:T(8,128)S(1)}, f32[1024,768]{0,1:T(8,128)}, u32[]{:S(2)}) copy-start(f32[1024,768]{0,1:T(8,128)} %copy-done.14) | copy-start | bytes 9437188
  350.9 10.9 %copy-start.76 = (bf16[1024,3072]{1,0:T(8,128)(2,1)S(1)}, bf16[1024,3072]{1,0:T(8,128)(2,1)}, u32[]{:S(2)}) copy-start(bf16[1024,3072]{1,0:T(8,128)(2,1)} %get-tuple-element.383) | copy-start | bytes 18874372
  361.8 5.6 copy-start.57
  379.6 271.8 %all-gather.8.cloned.1.call-start = ((), (), s32[]{:S(2)}) async-start(), calls=%async_computation.2 | async-start | bytes 4718592 | tf_op jit(solution)/shard_map/all_gather | solution.py:279
  405.3 7.1 copy-start.25
  431.0 7.1 copy-start.25
  539.8 8.7 %copy-start.32 = (bf16[3,6,128,128]{3,2,1,0:T(8,128)(2,1)S(1)}, bf16[3,6,128,128]{3,2,1,0:T(8,128)(2,1)}, u32[]{:S(2)}) copy-start(bf16[3,6,128,128]{3,2,1,0:T(8,128)(2,1)} %copy.222) | copy-start | bytes 1769476
  548.5 209.7 %reduce-scatter.2.cloned.1.call-start = ((), (), s32[]{:S(2)}) async-start(), calls=%async_computation.3 | async-start | bytes 15138816 | tf_op jit(solution)/shard_map/reduce_scatter | solution.py:328
  548.6 5.3 copy-start.33
  577.5 7.4 copy-start.75
  595.1 50.3 %copy-start.54 = (f32[6,768]{1,0:T(8,128)S(1)}, f32[6,768]{1,0:T(8,128)}, u32[]{:S(2)}) copy-start(f32[6,768]{1,0:T(8,128)} %param.33) | copy-start | bytes 55300
  595.1 50.3 %copy-start.59 = (f32[6,768]{1,0:T(8,128)S(1)}, f32[6,768]{1,0:T(8,128)}, u32[]{:S(2)}) copy-start(f32[6,768]{1,0:T(8,128)} %param.34) | copy-start | bytes 55300
  595.1 50.3 %copy-start.60 = (f32[6,768]{1,0:T(8,128)S(1)}, f32[6,768]{1,0:T(8,128)}, u32[]{:S(2)}) copy-start(f32[6,768]{1,0:T(8,128)} %param.35) | copy-start | bytes 55300
  595.1 50.9 %copy-start.58 = (f32[1,2304]{1,0:T(1,128)S(1)}, f32[1,2304]{1,0:T(1,128)}, u32[]{:S(2)}) copy-start(f32[1,2304]{1,0:T(1,128)} %param.30) | copy-start | bytes 27652
  595.2 50.9 %copy-start.69 = (f32[1,2304]{1,0:T(1,128)S(1)}, f32[1,2304]{1,0:T(1,128)}, u32[]{:S(2)}) copy-start(f32[1,2304]{1,0:T(1,128)} %param.31) | copy-start | bytes 27652
  595.2 50.9 %copy-start.70 = (f32[1,2304]{1,0:T(1,128)S(1)}, f32[1,2304]{1,0:T(1,128)}, u32[]{:S(2)}) copy-start(f32[1,2304]{1,0:T(1,128)} %param.32) | copy-start | bytes 27652
  651.4 106.8 %copy-start.40 = (f32[1,14,128,128]{3,2,1,0:T(8,128)S(1)}, f32[1,14,128,128]{3,2,1,0:T(8,128)}, u32[]{:S(2)}) copy-start(f32[1,14,128,128]{3,2,1,0:T(8,128)} %param.28) | copy-start | bytes 2752516
  651.4 109.4 %copy-start.41 = (f32[1,14,128,128]{3,2,1,0:T(8,128)S(1)}, f32[1,14,128,128]{3,2,1,0:T(8,128)}, u32[]{:S(2)}) copy-start(f32[1,14,128,128]{3,2,1,0:T(8,128)} %param.27) | copy-start | bytes 2752516
  (65 other events, 202.8 us)
Sparse Core Ops, SparseCore 0:
  11.4 108.0 all-gather.9
  379.7 43.0 all-gather.5
  548.6 43.0 all-gather.7
  593.9 164.2 reduce-scatter.1

commit v2 on v0

v2 whole, which is shorter than its diff:
```python
import jax
import jax.numpy as jnp
from jax import lax
from jax.experimental import pallas as pl
from jax.experimental.pallas import tpu as pltpu
from jax.sharding import PartitionSpec as P
import numpy as np

D = 768
HEADS = 12
HEAD = 64
FF = 3072


EPS_NORM = 1e-05
EPS_ADAM = 1e-08
LEARN_RATE = 0.01
VECTOR_RATE = 0.15
MOMENT_DECAY = 0.5
MASKED_SCORE = -1e30
HIGHEST_PRECISION = lax.Precision.HIGHEST


def slot_table(block_of_slot, block_total):
    slot_numbers = jnp.arange(block_of_slot.shape[0], dtype=jnp.int32)
    matches = block_of_slot[:, None] == jnp.arange(block_total, dtype=jnp.int32)[None, :]
    return jnp.sum(jnp.where(matches, slot_numbers[:, None], 0), axis=0)


def block_counts(block_edge, head_width, ffn_width):
    return (
        D // block_edge * (3 * head_width // block_edge),
        head_width // block_edge * (D // block_edge),
        D // block_edge * (ffn_width // block_edge),
        ffn_width // block_edge * (D // block_edge),
    )


def rotate_update(gradient, moment_one, moment_two, left, right, master):
    turned = jnp.einsum("psji,psjk->psik", left, gradient, precision=HIGHEST_PRECISION)
    turned = jnp.einsum("psik,pskl->psil", turned, right, precision=HIGHEST_PRECISION)
    first_new = MOMENT_DECAY * moment_one + (1.0 - MOMENT_DECAY) * turned
    second_new = MOMENT_DECAY * moment_two + (1.0 - MOMENT_DECAY) * turned * turned
    stepped = first_new / (jnp.sqrt(second_new) + EPS_ADAM)
    turned_back = jnp.einsum("psij,psjk->psik", left, stepped, precision=HIGHEST_PRECISION)
    turned_back = jnp.einsum("psik,pslk->psil", turned_back, right, precision=HIGHEST_PRECISION)
    return (master - LEARN_RATE * turned_back, first_new, second_new)


def adam_vector(gradient, moment_one, moment_two, current):
    first_new = MOMENT_DECAY * moment_one + (1.0 - MOMENT_DECAY) * gradient
    second_new = MOMENT_DECAY * moment_two + (1.0 - MOMENT_DECAY) * gradient * gradient
    return (
        current - VECTOR_RATE * first_new / (jnp.sqrt(second_new) + EPS_ADAM),
        first_new,
        second_new,
    )


LOG2E = 1.4426950408889634
LN_TWO = 0.6931471805599453
ROOT_HALF = 0.7071067811865476
PHI_SCALE = 0.3989422804014327
ERF_P = 0.3275911
ERF_A = (0.254829592, -0.284496736, 1.421413741, -1.453152027, 1.061405429)
VMEM_LIMIT = 60 * 1024 * 1024
LANES = 128
BF16 = jnp.bfloat16
F32 = jnp.float32


def dot_nn(left, right):
    return lax.dot_general(left, right, (((1,), (0,)), ((), ())), preferred_element_type=F32)


def dot_nt(left, right):
    return lax.dot_general(left, right, (((1,), (1,)), ((), ())), preferred_element_type=F32)


def dot_tn(left, right):
    return lax.dot_general(left, right, (((0,), (0,)), ((), ())), preferred_element_type=F32)


def block_home(pieces):
    d_b, f_b = D // LANES, FF // LANES
    d_p, f_p = d_b // pieces, f_b // pieces
    first = d_b * 3 * d_p
    second = first + d_p * d_b
    third = second + d_b * f_p
    qkv = [
        (n % d_b // d_p, k * 3 * d_p + n // d_b * d_p + n % d_p)
        for k in range(d_b)
        for n in range(3 * d_b)
    ]
    out = [(k // d_p, first + k % d_p * d_b + n) for k in range(d_b) for n in range(d_b)]
    up = [(n // f_p, second + k * f_p + n % f_p) for k in range(d_b) for n in range(f_b)]
    down = [(k // f_p, third + k % f_p * d_b + n) for k in range(f_b) for n in range(d_b)]
    return qkv, out, up, down


def grad_order(pieces):
    d_b, f_b = D // LANES, FF // LANES
    qkv, out, up, down = block_home(pieces)
    f_s, q_s = f_b // d_b, 3
    order = []
    for j in range(d_b):
        order += [down[(j * f_s + k) * d_b + n] for k in range(f_s) for n in range(d_b)]
        order += [up[k * f_b + j * f_s + n] for k in range(d_b) for n in range(f_s)]
        order += [qkv[k * 3 * d_b + j * q_s + n] for k in range(d_b) for n in range(q_s)]
        order += [out[j * d_b + n] for n in range(d_b)]
    return order


def start_blocks(homes, base, rows, cols, source, target, sem):
    def step(index, carry):
        k, n = index // cols, index % cols
        pltpu.make_async_copy(
            source.at[homes[base + index]],
            target.at[pl.ds(pl.multiple_of(k * LANES, LANES), LANES), pl.ds(pl.multiple_of(n * LANES, LANES), LANES)],
            sem,
        ).start()
        return carry

    lax.fori_loop(0, rows * cols, step, 0, unroll=6)


def wait_blocks(target, sem):
    pltpu.make_async_copy(target, target, sem).wait()


def mask_bias(ends_ref, row, seq, bias_ref):
    col = lax.broadcasted_iota(jnp.int32, (seq, 1), 0)
    lane = lax.broadcasted_iota(jnp.int32, (1, seq), 1)
    seg_col = jnp.zeros((seq, 1), jnp.int32)
    seg_lane = jnp.zeros((1, seq), jnp.int32)
    end = 0
    for k in range(ends_ref.shape[1] - 1):
        end = end + ends_ref[row, k]
        seg_col = seg_col + (col >= end).astype(jnp.int32)
        seg_lane = seg_lane + (lane >= end).astype(jnp.int32)
    bias_ref[...] = jnp.where(seg_col == seg_lane, 0.0, MASKED_SCORE)


def attend_kernel(homes, pairs, offset, x_ref, every, qb_ref, vb_ref, qkv_ref, att_ref, lse_ref, w_ref, bias_ref, sem):
    d_b = D // LANES
    row = pl.program_id(0)
    seq = x_ref.shape[0]

    @pl.when(row == 0)
    def _():
        start_blocks(homes, 0, d_b, 3 * d_b, every, w_ref, sem)

    mask_bias(pairs, offset[0] + row, seq, bias_ref)

    @pl.when(row == 0)
    def _():
        wait_blocks(w_ref, sem)

    x = x_ref[...]
    wide = 2 * LANES
    for part in range(3):
        for c in range(0, D, wide):
            y = dot_nn(x, w_ref[:, part * D + c : part * D + c + wide])
            if part == 0:
                y = (y + qb_ref[:, c : c + wide]).astype(BF16).astype(F32) * HEAD ** (-0.5)
            if part == 2:
                y = y + vb_ref[:, c : c + wide]
            y = y.astype(BF16)
            for n in range(2):
                qkv_ref[part * d_b + c // LANES + n] = y[:, n * LANES : (n + 1) * LANES]
    lane = lax.broadcasted_iota(jnp.int32, (1, LANES), 1)

    def pair(n, carry):
        q = qkv_ref[n]
        k = qkv_ref[d_b + n]
        v_t = qkv_ref[2 * d_b + n].T
        halves = []
        for h in range(2):
            keep = (lane < HEAD) if h == 0 else (lane >= HEAD)
            scores = dot_nt(jnp.where(keep, k, jnp.zeros_like(k)), q) + bias_ref[...]
            top = jnp.max(scores, axis=0, keepdims=True)
            p = jnp.exp(scores - top)
            total = jnp.sum(p, axis=0, keepdims=True)
            lse_ref[0, 2 * n + h] = (top + jnp.log(total)).reshape(1, seq)
            mixed = dot_nn(v_t[h * HEAD : (h + 1) * HEAD], p.astype(BF16))
            halves.append(mixed * (1.0 / total))
        att_ref[n] = jnp.concatenate(halves, axis=0).T.astype(BF16)
        return carry

    lax.fori_loop(0, d_b, pair, 0)


def norm_parts(hidden):
    mean = jnp.mean(hidden, axis=-1, keepdims=True)
    centred = hidden - mean
    var = jnp.mean(centred * centred, axis=-1, keepdims=True)
    inv = lax.rsqrt(var + EPS_NORM)
    return centred * inv, inv


def norm_back(grad, gain, normed, inv):
    scaled = grad * gain
    mean = jnp.mean(scaled, axis=-1, keepdims=True)
    along = jnp.mean(scaled * normed, axis=-1, keepdims=True)
    return inv * (scaled - mean - normed * along)


def put_blocks(ref, value):
    for n in range(ref.shape[0]):
        ref[n] = value[:, n * LANES : (n + 1) * LANES]


def get_blocks(ref):
    return jnp.concatenate([ref[n] for n in range(ref.shape[0])], axis=1)


def gelu_parts(u):
    e = jnp.exp(u * u * -0.5)
    t = 1.0 / (1.0 + (ERF_P * ROOT_HALF) * jnp.abs(u))
    a1, a2, a3, a4, a5 = (0.5 * a for a in ERF_A)
    tail = ((((a5 * t + a4) * t + a3) * t + a2) * t + a1) * t * e
    cdf = jnp.where(u >= 0, 1.0 - tail, tail)
    return u * cdf, cdf + u * e * PHI_SCALE


def token_kernel(
    homes, att_ref, x_ref, cot_ref, every, bu_ref, rv_ref,
    out_ref, nl_ref, act_ref, dl_ref, up_ref, al_ref, ml_ref, g1_ref, rg_ref, bg_ref,
    wo_ref, wu_ref, wd_ref, dg_ref, sem,
):
    d_b, f_b = D // LANES, FF // LANES
    step = pl.program_id(0)

    @pl.when(step == 0)
    def _():
        start_blocks(homes, 3 * d_b * d_b, d_b, d_b, every, wo_ref, sem.at[0])
        start_blocks(homes, 4 * d_b * d_b, d_b, f_b, every, wu_ref, sem.at[1])
        start_blocks(homes, 4 * d_b * d_b + d_b * f_b, f_b, d_b, every, wd_ref, sem.at[2])
        rg_ref[...] = jnp.zeros_like(rg_ref)
        bg_ref[...] = jnp.zeros_like(bg_ref)
        wait_blocks(wo_ref, sem.at[0])
        wait_blocks(wu_ref, sem.at[1])
        wait_blocks(wd_ref, sem.at[2])

    out_bias, gain_one, shift_one, down_bias, gain_two, shift_two = (
        rv_ref[i : i + 1] for i in range(6)
    )
    hidden = dot_nn(get_blocks(att_ref), wo_ref[...]) + x_ref[...].astype(F32) + out_bias
    n_one, inv_one = norm_parts(hidden)
    normed = n_one * gain_one + shift_one
    normed_low = normed.astype(BF16)
    put_blocks(nl_ref, normed_low)
    wide = 512
    total = normed + down_bias
    for c in range(0, FF, wide):
        u = dot_nn(normed_low, wu_ref[:, c : c + wide]) + bu_ref[:, c : c + wide]
        active, slope = gelu_parts(u)
        active = active.astype(BF16)
        dg_ref[:, c : c + wide] = slope.astype(BF16)
        for n in range(wide // LANES):
            act_ref[c // LANES + n] = active[:, n * LANES : (n + 1) * LANES]
        total = total + dot_nn(active, wd_ref[c : c + wide, :])
    n_two, inv_two = norm_parts(total)
    out_ref[...] = (n_two * gain_two + shift_two).astype(BF16)
    dy = cot_ref[...].astype(F32)
    grad_two = norm_back(dy, gain_two, n_two, inv_two)
    down_low = grad_two.astype(BF16)
    put_blocks(dl_ref, down_low)
    rg_ref[3:4] += jnp.sum(grad_two, axis=0, keepdims=True)
    rg_ref[4:5] += jnp.sum(dy * n_two, axis=0, keepdims=True)
    rg_ref[5:6] += jnp.sum(dy, axis=0, keepdims=True)
    grad_normed = grad_two
    for c in range(0, FF, wide):
        ga = dot_nt(down_low, wd_ref[c : c + wide, :]) * dg_ref[:, c : c + wide].astype(F32)
        up = ga.astype(BF16)
        for n in range(wide // LANES):
            up_ref[c // LANES + n] = up[:, n * LANES : (n + 1) * LANES]
        bg_ref[:, c : c + wide] += jnp.sum(up.astype(F32), axis=0, keepdims=True)
        grad_normed = grad_normed + dot_nt(up, wu_ref[:, c : c + wide])
    rg_ref[1:2] += jnp.sum(grad_normed * n_one, axis=0, keepdims=True)
    rg_ref[2:3] += jnp.sum(grad_normed, axis=0, keepdims=True)
    grad_one = norm_back(grad_normed, gain_one, n_one, inv_one)
    rg_ref[0:1] += jnp.sum(grad_one, axis=0, keepdims=True)
    g1_ref[...] = grad_one
    attn_low = grad_one.astype(BF16)
    put_blocks(al_ref, attn_low)
    put_blocks(ml_ref, dot_nt(attn_low, wo_ref[...]).astype(BF16))


def attend_back_kernel(
    homes, pairs, offset, qkv_ref, att_ref, ml_ref, lse_ref, g1_ref, every,
    merged_ref, ig_ref, sg_ref, w_ref, bias_ref, sem,
):
    d_b = D // LANES
    row = pl.program_id(0)
    seq = g1_ref.shape[0]

    @pl.when(row == 0)
    def _():
        start_blocks(homes, 0, d_b, 3 * d_b, every, w_ref, sem)
        sg_ref[...] = jnp.zeros_like(sg_ref)

    mask_bias(pairs, offset[0] + row, seq, bias_ref)
    lane = lax.broadcasted_iota(jnp.int32, (1, LANES), 1)

    def pair(n, carry):
        q = qkv_ref[n]
        k = qkv_ref[d_b + n]
        v = qkv_ref[2 * d_b + n]
        g = ml_ref[n]
        k_t = k.T
        both = g.T.astype(F32) * att_ref[n].T.astype(F32)
        zero = jnp.zeros_like(k)
        parts = []
        for h in range(2):
            keep = (lane < HEAD) if h == 0 else (lane >= HEAD)
            spread = jnp.sum(both[h * HEAD : (h + 1) * HEAD], axis=0, keepdims=True)
            scores = dot_nt(jnp.where(keep, k, zero), q) + bias_ref[...]
            p = jnp.exp(scores - lse_ref[0, 2 * n + h].reshape(1, seq))
            gp = dot_nt(jnp.where(keep, v, zero), g)
            low = (p * (gp - spread)).astype(BF16)
            gv = dot_nn(p.astype(BF16), g)
            gk = dot_nn(low, q)
            gq = dot_nn(k_t[h * HEAD : (h + 1) * HEAD], low)
            parts.append((gq, gk, gv))
        gq = (jnp.concatenate([parts[0][0], parts[1][0]], axis=0) * HEAD ** (-0.5)).T
        merged_ref[n] = gq.astype(BF16)
        merged_ref[d_b + n] = jnp.where(lane < HEAD, parts[0][1], parts[1][1]).astype(BF16)
        merged_ref[2 * d_b + n] = jnp.where(lane < HEAD, parts[0][2], parts[1][2]).astype(BF16)
        return carry

    lax.fori_loop(0, d_b, pair, 0)

    @pl.when(row == 0)
    def _():
        wait_blocks(w_ref, sem)

    for n in range(d_b):
        at = slice(n * LANES, (n + 1) * LANES)
        sg_ref[0:1, at] += jnp.sum(merged_ref[n].astype(F32), axis=0, keepdims=True)
        sg_ref[1:2, at] += jnp.sum(merged_ref[2 * d_b + n].astype(F32), axis=0, keepdims=True)
    merged = get_blocks(merged_ref)
    ig_ref[...] = (g1_ref[...] + dot_nt(merged, w_ref[...])).astype(BF16)


def grad_kernel(act_ref, dl_ref, nl_ref, up_ref, x_ref, merged_ref, att_ref, al_ref, g_ref):
    d_b = D // LANES
    f_s = act_ref.shape[0]
    at = 0

    def store(value, at):
        value = value.astype(BF16)
        for k in range(value.shape[0] // LANES):
            for n in range(value.shape[1] // LANES):
                g_ref[at] = value[k * LANES : (k + 1) * LANES, n * LANES : (n + 1) * LANES]
                at += 1
        return at

    at = store(dot_tn(get_blocks(act_ref), get_blocks(dl_ref)), at)
    at = store(dot_tn(get_blocks(nl_ref), get_blocks(up_ref)), at)
    at = store(dot_tn(x_ref[...], get_blocks(merged_ref)), at)
    at = store(dot_tn(att_ref[0], get_blocks(al_ref)), at)


def slot_kernel(places, g_ref, zero_ref, out_ref, sem):
    def step(s, carry):
        @pl.when(places[s] >= 0)
        def _():
            pltpu.make_async_copy(g_ref.at[jnp.maximum(places[s], 0)], out_ref.at[s], sem).start()

        @pl.when(places[s] < 0)
        def _():
            pltpu.make_async_copy(zero_ref.at[0], out_ref.at[s], sem).start()

        return carry

    lax.fori_loop(0, places.shape[0], step, 0)
    pltpu.make_async_copy(out_ref, out_ref, sem).wait()


def smem():
    return pl.BlockSpec(memory_space=pltpu.SMEM)


def anywhere():
    return pl.BlockSpec(memory_space=pl.ANY)


def params():
    return pltpu.CompilerParams(vmem_limit_bytes=VMEM_LIMIT, dimension_semantics=("arbitrary",))


def layer_passes(tokens, cotangent, pair_lengths, piece, homes, every, query_bias, value_bias, up_bias, row_vec, row_count, seq):
    d_b, f_b = D // LANES, FF // LANES
    total = row_count * seq
    shape = jax.ShapeDtypeStruct
    offset = (piece * row_count).astype(jnp.int32).reshape(1)
    stack = lambda n: pl.BlockSpec((n, seq, LANES), lambda r, *_: (0, r, 0))
    rows = pl.BlockSpec((seq, D), lambda r, *_: (r, 0))
    own = lambda at: pl.BlockSpec((seq, D), lambda r, *pre: (pre[at][0] + r, 0))
    whole = lambda s: pl.BlockSpec(s, lambda *_: tuple(0 for _ in s))
    lse_spec = pl.BlockSpec((1, HEADS, 1, seq), lambda r, *_: (r, 0, 0, 0))
    qkv, att, lse = pl.pallas_call(
        attend_kernel,
        grid_spec=pltpu.PrefetchScalarGridSpec(
            num_scalar_prefetch=3,
            grid=(row_count,),
            in_specs=[own(2), anywhere(), whole((1, D)), whole((1, D))],
            out_specs=[stack(3 * d_b), stack(d_b), lse_spec],
            scratch_shapes=[
                pltpu.VMEM((D, 3 * D), BF16),
                pltpu.VMEM((seq, seq), F32),
                pltpu.SemaphoreType.DMA,
            ],
        ),
        out_shape=[
            shape((3 * d_b, total, LANES), BF16),
            shape((d_b, total, LANES), BF16),
            shape((row_count, HEADS, 1, seq), F32),
        ],
        compiler_params=params(),
        name="attend",
    )(homes, pair_lengths, offset, tokens, every, query_bias, value_bias)
    token_outs = pl.pallas_call(
        lambda homes, off, *refs: token_kernel(homes, *refs),
        grid_spec=pltpu.PrefetchScalarGridSpec(
            num_scalar_prefetch=2,
            grid=(row_count,),
            in_specs=[stack(d_b), own(1), own(1), anywhere(), whole((1, FF)), whole((6, D))],
            out_specs=[
                rows, stack(d_b), stack(f_b), stack(d_b), stack(f_b), stack(d_b), stack(d_b), rows,
                whole((6, D)), whole((1, FF)),
            ],
            scratch_shapes=[
                pltpu.VMEM((D, D), BF16),
                pltpu.VMEM((D, FF), BF16),
                pltpu.VMEM((FF, D), BF16),
                pltpu.VMEM((seq, FF), BF16),
                pltpu.SemaphoreType.DMA((3,)),
            ],
        ),
        out_shape=[
            shape((total, D), BF16),
            shape((d_b, total, LANES), BF16),
            shape((f_b, total, LANES), BF16),
            shape((d_b, total, LANES), BF16),
            shape((f_b, total, LANES), BF16),
            shape((d_b, total, LANES), BF16),
            shape((d_b, total, LANES), BF16),
            shape((total, D), F32),
            shape((6, D), F32),
            shape((1, FF), F32),
        ],
        compiler_params=params(),
        name="tokenwise",
    )(homes, offset, att, tokens, cotangent, every, up_bias, row_vec)
    layer_own, normed_low, active_low, down_low, up_low, attn_low, mixed_low, grad_one, row_grad, up_grad = token_outs
    merged, input_own, split_grad = pl.pallas_call(
        attend_back_kernel,
        grid_spec=pltpu.PrefetchScalarGridSpec(
            num_scalar_prefetch=3,
            grid=(row_count,),
            in_specs=[stack(3 * d_b), stack(d_b), stack(d_b), lse_spec, rows, anywhere()],
            out_specs=[stack(3 * d_b), rows, whole((2, D))],
            scratch_shapes=[
                pltpu.VMEM((D, 3 * D), BF16),
                pltpu.VMEM((seq, seq), F32),
                pltpu.SemaphoreType.DMA,
            ],
        ),
        out_shape=[
            shape((3 * d_b, total, LANES), BF16),
            shape((total, D), BF16),
            shape((2, D), F32),
        ],
        compiler_params=params(),
        name="attend_back",
    )(homes, pair_lengths, offset, qkv, att, mixed_low, lse, grad_one, every)
    f_s = f_b // d_b
    part = lambda n: pl.BlockSpec((n, total, LANES), lambda j, *_: (j, 0, 0))
    blocks = 2 * f_s * d_b + 4 * d_b
    grads = pl.pallas_call(
        lambda pc, *refs: grad_kernel(*refs),
        grid_spec=pltpu.PrefetchScalarGridSpec(
            num_scalar_prefetch=1,
            grid=(d_b,),
            in_specs=[
                part(f_s), whole((d_b, total, LANES)), whole((d_b, total, LANES)), part(f_s),
                pl.BlockSpec((total, D), lambda j, pc: (pc[0], 0)),
                part(3), part(1), whole((d_b, total, LANES)),
            ],
            out_specs=pl.BlockSpec((blocks, LANES, LANES), lambda j, *_: (j, 0, 0)),
        ),
        out_shape=shape((d_b * blocks, LANES, LANES), BF16),
        compiler_params=params(),
        name="weight_grads",
    )(piece.astype(jnp.int32).reshape(1), active_low, down_low, normed_low, up_low, tokens, merged, att, attn_low)
    return layer_own, input_own, grads, row_grad, up_grad, split_grad


def body(
    tokens,
    cotangent,
    pair_lengths,
    block_of_slot,
    masters,
    mom_first,
    mom_second,
    left_bases,
    right_bases,
    split_vec,
    split_first,
    split_second,
    row_vec,
    row_first,
    row_second,
):
    pieces = lax.axis_size("tensor")
    piece = lax.axis_index("tensor")
    piece_width = HEADS * HEAD // pieces
    piece_ffn = FF // pieces
    block_edge = masters.shape[-1]
    block_total = sum(block_counts(block_edge, piece_width, piece_ffn))
    slots = block_of_slot.shape[0]
    full_seq = tokens.shape[0] // pair_lengths.shape[0]
    row_count = pair_lengths.shape[0] // pieces
    every = lax.all_gather(masters[0].astype(BF16), ("tensor", "dp"), axis=0, tiled=True)
    slot_of = slot_table(block_of_slot, block_total)
    order = np.array(sum(block_home(pieces), []), np.int32)
    homes = slot_of[order[:, 1]] + order[:, 0] * slots
    split_all = lax.all_gather(split_vec[0], "tensor", axis=0)
    query_bias = split_all[:, :piece_width].reshape(1, -1)
    value_bias = split_all[:, piece_width : 2 * piece_width].reshape(1, -1)
    up_bias = split_all[:, 2 * piece_width :].reshape(1, -1)
    layer_own, input_own, grads, row_local, up_grad, qv_grad = layer_passes(
        tokens, cotangent, pair_lengths, piece, homes, every, query_bias, value_bias, up_bias, row_vec, row_count, full_seq
    )
    layer_out = lax.all_gather(layer_own, "tensor", axis=0, tiled=True)
    input_grad = lax.all_gather(input_own, "tensor", axis=0, tiled=True).astype(F32)
    place_table = np.full((pieces, block_total + 1), -1, np.int32)
    for index, (at_piece, number) in enumerate(grad_order(pieces)):
        place_table[at_piece, number] = index
    places = jnp.asarray(place_table)[:, block_of_slot].reshape(-1)
    slot_terms = pl.pallas_call(
        slot_kernel,
        in_specs=[smem(), anywhere(), anywhere()],
        out_specs=anywhere(),
        out_shape=jax.ShapeDtypeStruct((pieces * slots, block_edge, block_edge), BF16),
        scratch_shapes=[pltpu.SemaphoreType.DMA],
        name="slots",
    )(places, grads, jnp.zeros((1, block_edge, block_edge), BF16))
    split_local = jnp.concatenate(
        [
            qv_grad[0].reshape(pieces, piece_width),
            qv_grad[1].reshape(pieces, piece_width),
            up_grad.reshape(pieces, piece_ffn),
        ],
        axis=1,
    )
    token_total = tokens.shape[0] * lax.axis_size("dp")
    mean_scale = 1.0 / token_total
    owned_sum = lax.psum_scatter(
        slot_terms, ("tensor", "dp"), scatter_dimension=0, tiled=True
    ).astype(F32)
    split_total, row_total = lax.psum((split_local, row_local), ("tensor", "dp"))
    weight_grads = (owned_sum * mean_scale)[None]
    split_grad = lax.dynamic_slice_in_dim(split_total, piece, 1, 0) * mean_scale
    row_grad = row_total * mean_scale
    new_masters, new_first, new_second = rotate_update(
        weight_grads, mom_first, mom_second, left_bases, right_bases, masters
    )
    new_split, new_split_first, new_split_second = adam_vector(
        split_grad, split_first, split_second, split_vec
    )
    new_row, new_row_first, new_row_second = adam_vector(row_grad, row_first, row_second, row_vec)
    return (
        layer_out,
        input_grad,
        weight_grads,
        new_masters,
        new_first,
        new_second,
        new_masters.astype(jnp.bfloat16),
        split_grad,
        new_split,
        new_split_first,
        new_split_second,
        row_grad,
        new_row,
        new_row_first,
        new_row_second,
    )


def solution(mesh):
    in_specs = (
        P("dp", None),
        P("dp", None),
        P("dp", None),
        P(),
        P("tensor", "dp", None, None),
        P("tensor", "dp", None, None),
        P("tensor", "dp", None, None),
        P("tensor", "dp", None, None),
        P("tensor", "dp", None, None),
        P("tensor", None),
        P("tensor", None),
        P("tensor", None),
        P(),
        P(),
        P(),
    )
    out_specs = (
        P("dp", None),
        P("dp", None),
        P("tensor", "dp", None, None),
        P("tensor", "dp", None, None),
        P("tensor", "dp", None, None),
        P("tensor", "dp", None, None),
        P("tensor", "dp", None, None),
        P("tensor", None),
        P("tensor", None),
        P("tensor", None),
        P("tensor", None),
        P(),
        P(),
        P(),
        P(),
    )
    return jax.shard_map(body, mesh=mesh, in_specs=in_specs, out_specs=out_specs, check_vma=False)
```

time: 974 us -> 878 us (0.901)
  Pallas kernels: 0 us -> 573 us
  waiting for transfers between devices: 418 us -> 207 us
  matrix products: 210 us -> 9.45 us
  local copies, waits for them, and re-layouts: 159 us -> 11.3 us
  other arithmetic: 96.8 us -> 12.4 us
  blocking collectives: 63.2 us -> 50.5 us
    pallas_call x0 -> x5, Pallas kernels: none -> 573 us  [the longest x1 447 us: body(): pl.pallas_call(slot_kernel, in_specs=[smem(), anywhere(), anywhere()], ou...]
    psum x4 -> x0, waiting for transfers between devices: 267 us -> none  [the longest x1 85.9 us: body(): lax.psum(down_part.astype(jnp.bfloat16), 'tensor').astype(jnp.float32)]
    dot_general x40 -> x0, matrix products: 200 us -> none  [the longest x1 35.6 us: body(): jnp.dot(normed_low, w_up, preferred_element_type=jnp.float32) + up_bias]
    reduce_sum x15 -> x0, other arithmetic: 50.8 us -> none  [the longest x2 13.6 us: norm_row(): return centred * lax.rsqrt(row_var + EPS_NORM) * gain_vec + shift_vec]
    reshape x15 -> x2, local copies, waits for them, and re-layouts: 41.1 us -> 0.69 us  [the longest x1 0.68 us: body(): places = jnp.asarray(place_table)[:, block_of_slot].reshape(-1)]
    all_gather x1 -> x3, waiting for transfers between devices: 69.9 us -> 97.6 us  [the longest x1 97.6 us: body(): lax.all_gather(masters[0].astype(BF16), ('tensor', 'dp'), axis=0, tiled=T...]
    reduce_scatter x1, waiting for transfers between devices: 81.2 us -> 108 us  [body(): lax.psum_scatter(slot_terms, ('tensor', 'dp'), scatter_dimension=0, tiled...]
    gather x2 -> x3, local copies, waits for them, and re-layouts: 28 us -> 4.84 us  [the longest x1 3.16 us: body(): homes = slot_of[order[:, 1]] + order[:, 0] * slots]
  transfers between devices with their start and end apart: 6 -> 4, of which waited for: 6 -> 2; matrix products, arithmetic and copies ran while one was open for 8% -> 2% of each run, Pallas kernels for 0% -> 54%
where the time goes in v2:
time: 878 us; the launch traced here: 877 us
  Pallas kernels  573 us (65%)
  waiting for transfers between devices  207 us (24%)
  blocking collectives  50.5 us (6%)
  between operations  14.1 us (2%)
  other arithmetic  12.4 us (1%)
  local copies, waits for them, and re-layouts  11.3 us (1%)
  matrix products  9.45 us (1%)
    pallas_call x1, Pallas kernels, body(): pl.pallas_call(slot_kernel, in_specs=[smem(), anywhere(), anywhere()], ou...  447 us
    reduce_scatter x1, waiting for transfers between devices, body(): lax.psum_scatter(slot_terms, ('tensor', 'dp'), scatter_dimension=0, tiled...  108 us
    all_gather x1, waiting for transfers between devices, body(): lax.all_gather(masters[0].astype(BF16), ('tensor', 'dp'), axis=0, tiled=T...  97.6 us
    pallas_call x1, Pallas kernels, layer_passes(): pl.pallas_call(lambda homes, off, *refs: token_kernel(homes, *refs), grid...  48.2 us
    psum x1, blocking collectives, body(): lax.psum((split_local, row_local), ('tensor', 'dp'))  45 us
    pallas_call x1, Pallas kernels, layer_passes(): pl.pallas_call(attend_back_kernel, grid_spec=pltpu.PrefetchScalarGridSpec...  29.5 us
    pallas_call x1, Pallas kernels, layer_passes(): pl.pallas_call(attend_kernel, grid_spec=pltpu.PrefetchScalarGridSpec(num_...  24.6 us
    pallas_call x1, Pallas kernels, layer_passes(): pl.pallas_call(lambda pc, *refs: grad_kernel(*refs), grid_spec=pltpu.Pref...  23.8 us
  transfers between devices with their start and end apart: 4, of which 2 were waited for; matrix products, arithmetic and copies ran while one was open for 2% of the time, Pallas kernels for 54%

profile of v2, /device:TPU:0, one launch (start us, length us, event | category | flops | bytes accessed | tf_op | source)
XLA Modules:
  0.0 877.3 jit_solution(2627364324244052086)
XLA Ops:
  7.3 2.1 bitcast_convert_fusion
  9.4 5.5 all-gather.1
  15.0 0.6 copy.52
  15.6 0.6 copy.53
  16.2 0.6 copy.54
  16.8 0.7 pad_clamp_fusion.1
  17.5 0.8 select_reduce_fusion
  18.3 3.2 gather_fusion
  21.4 0.6 add.62.homes
  22.0 97.6 %all-gather.10.cloned.1.call-done = bf16[1,448,128,128]{3,2,0,1:T(8,128)(2,1)} async-done(((bf16[1,14,128,128]{3,2,0,1:T(8,128)(2,1)}), bf16[1,448,128,128]{3,2,0,1:T(8,128)(2,1)}) %all-gather.10.cloned.1.call-update) | async-done | bytes 14680080 | tf_op jit(solution)/shard_map/all_gather | solution.py:527
  119.7 24.6 %attend.1 = (bf16[18,1024,128]{2,1,0:T(8,128)(2,1)}, bf16[6,1024,128]{2,1,0:T(8,128)(2,1)}, f32[2,12,1,512]{3,2,1,0:T(1,128)}) custom-call(s32[432]{0:T(512)} %add.62.homes, s32[4,4]{1,0:T(4,128)} %pairs.3, s32[1]{0:T(128)} %bitcast.offset.off, bf16[2048,768]{1,0:T(8,128)(2,1)} %refs_4_.1, bf16[448,128,128]{2,1,0:T(8,128)(2,1)} %bitcast.55, ...), custom_call_target="tpu_custom_call" | custom-call | tf_op jit(solution)/shard_map/attend/pallas_call | solution.py:403
  144.3 48.2 %tokenwise.1 = (bf16[1024,768]{1,0:T(8,128)(2,1)}, bf16[6,1024,128]{2,1,0:T(8,128)(2,1)}, bf16[24,1024,128]{2,1,0:T(8,128)(2,1)}, bf16[6,1024,128]{2,1,0:T(8,128...) custom-call(s32[432]{0:T(512)} %add.62.homes, ...), custom_call_target="tpu_custom_call" | custom-call | tf_op jit(solution)/shard_map/tokenwise/pallas_call | solution.py:424
  192.4 29.5 %attend_back.1 = (bf16[18,1024,128]{2,1,0:T(8,128)(2,1)}, bf16[1024,768]{1,0:T(8,128)(2,1)}, f32[2,768]{1,0:T(2,128)}) custom-call(s32[432]{0:T(512)} %add.62.homes, s32[4,4]{1,0:T(4,128)} %pairs.3, s32[1]{0:T(128)} %bitcast.offset.off, bf16[18,1024,128]{2,1,0:T(8,128)(2,1)} %get-tuple-element.33.qkv_ref, ...), custom_call_target="tpu_custom_call" | custom-call | tf_op jit(solution)/shard_map/attend_back/pallas_call | solution.py:458
  222.0 0.7 all-gather.6.cloned.1.call-update
  222.8 1.6 gather_fusion.1
  224.5 0.7 reshape.81.places
  225.2 23.8 %weight_grads.1.g_ref = bf16[432,128,128]{2,1,0:T(8,128)(2,1)} custom-call(s32[1]{0:T(128)} %bitcast.5.pc, bf16[24,1024,128]{2,1,0:T(8,128)(2,1)} %get-tuple-element.38.refs_0_, bf16[6,1024,128]{2,1,0:T(8,128)(2,1)} %get-tuple-element.39.refs_1_, bf16[6,1024,128]{2,1,0:T(8,128)(2,1)} %get-tuple-element.40.refs_2_, ...), custom_call_target="tpu_custom_call" | custom-call | tf_op jit(solution)/shard_map/weight_grads/pallas_call | solution.py:482
  249.0 0.6 broadcast_in_dim.31.zero_ref
  249.6 446.5 %slots.1 = bf16[448,128,128]{2,1,0:T(8,128)(2,1)} custom-call(s32[448]{0:T(512)} %reshape.81.places, bf16[432,128,128]{2,1,0:T(8,128)(2,1)} %weight_grads.1.g_ref, bf16[1,128,128]{2,1,0:T(8,128)(2,1)} %broadcast_in_dim.31.zero_ref), custom_call_target="tpu_custom_call" | custom-call | tf_op jit(solution)/shard_map/slots/pallas_call | solution.py:544
  696.2 0.6 copy-done.16
  697.4 0.7 reduce.7
  698.1 45.0 %all-reduce = (f32[2,2304]{1,0:T(2,128)S(1)}, f32[6,768]{1,0:T(8,128)S(1)}) all-reduce(f32[2,2304]{1,0:T(2,128)S(1)} %pad_maximum_fusion, f32[6,768]{1,0:T(8,128)S(1)} %copy-done.12), channel_id=1, replica_groups=mesh['dp'=16,'tensor'=2] {'tensor','dp'}, use_global_device_ids=true, to_apply=%region_2.3 | all-reduce | flops 9216 | bytes 73728 | tf_op jit(solution)/shard_map/psum | solution.py:565
  743.1 0.6 divide_subtract_fusion
  743.8 0.7 divide_subtract_fusion.1
  744.4 5.2 convert_element_type.17
  749.7 108.3 %reduce-scatter.2.cloned.1.call-done = bf16[14,128,128]{2,1,0:T(8,128)(2,1)} async-done(((bf16[448,128,128]{2,1,0:T(8,128)(2,1)}), bf16[14,128,128]{2,1,0:T(8,128)(2,1)}) %reduce-scatter.2.cloned.1.call-update) | async-done | bytes 458768 | tf_op jit(solution)/shard_map/reduce_scatter | solution.py:562
  858.0 2.6 fusion.11
  860.7 2.4 fusion.4
  863.1 1.3 fusion.5
  864.9 3.1 fusion.21
  868.0 1.0 fusion.16
  869.1 1.7 copy.58
  (58 shorter events, 1.5 us)
Async XLA Ops:
  7.2 853.5 %copy-start = (f32[1,14,128,128]{3,2,1,0:T(8,128)S(1)}, f32[1,14,128,128]{3,2,1,0:T(8,128)}, u32[]{:S(2)}) copy-start(f32[1,14,128,128]{3,2,1,0:T(8,128)} %param.27) | copy-start | bytes 2752516
  7.2 14.2 %copy-start.18 = (s32[432]{0:T(512)S(1)}, s32[432]{0:T(512)}, u32[]{:S(2)}) copy-start(s32[432]{0:T(512)} %constant.13.clone) | copy-start | bytes 5188
  7.2 112.4 %all-gather.10.cloned.1.call-start = ((), (), s32[]{:S(2)}) async-start(), calls=%async_computation.4 | async-start | bytes 15138816 | tf_op jit(solution)/shard_map/all_gather | solution.py:527
  9.4 735.1 %all-gather.8.cloned.1.call-start = ((), (), s32[]{:S(2)}) async-start(), calls=%async_computation.2 | async-start | bytes 4718592 | tf_op jit(solution)/shard_map/all_gather | solution.py:539
  221.9 0.8 copy-start.17
  222.0 527.7 %all-gather.6.cloned.1.call-start = ((), (), s32[]{:S(2)}) async-start(), calls=%async_computation.1 | async-start | bytes 4718592 | tf_op jit(solution)/shard_map/all_gather | solution.py:538
  222.7 635.3 %reduce-scatter.2.cloned.1.call-start = ((), (), s32[]{:S(2)}) async-start(), calls=%async_computation.3 | async-start | bytes 15138816 | tf_op jit(solution)/shard_map/reduce_scatter | solution.py:562
  696.1 0.7 copy-start.16
  696.1 1.2 copy-start.13
  696.1 2.0 copy-start.12
  696.1 46.9 %copy-start.8 = (f32[6,768]{1,0:T(8,128)S(1)}, f32[6,768]{1,0:T(8,128)}, u32[]{:S(2)}) copy-start(f32[6,768]{1,0:T(8,128)} %refs_5_.1) | copy-start | bytes 55300
  696.2 46.9 %copy-start.10 = (f32[6,768]{1,0:T(8,128)S(1)}, f32[6,768]{1,0:T(8,128)}, u32[]{:S(2)}) copy-start(f32[6,768]{1,0:T(8,128)} %param.32) | copy-start | bytes 55300
  696.2 46.9 %copy-start.11 = (f32[6,768]{1,0:T(8,128)S(1)}, f32[6,768]{1,0:T(8,128)}, u32[]{:S(2)}) copy-start(f32[6,768]{1,0:T(8,128)} %param.33) | copy-start | bytes 55300
  696.2 47.6 %copy-start.9 = (f32[1,2304]{1,0:T(1,128)S(1)}, f32[1,2304]{1,0:T(1,128)}, u32[]{:S(2)}) copy-start(f32[1,2304]{1,0:T(1,128)} %param.28) | copy-start | bytes 27652
  696.2 47.6 %copy-start.14 = (f32[1,2304]{1,0:T(1,128)S(1)}, f32[1,2304]{1,0:T(1,128)}, u32[]{:S(2)}) copy-start(f32[1,2304]{1,0:T(1,128)} %param.29) | copy-start | bytes 27652
  696.2 47.6 %copy-start.15 = (f32[1,2304]{1,0:T(1,128)S(1)}, f32[1,2304]{1,0:T(1,128)}, u32[]{:S(2)}) copy-start(f32[1,2304]{1,0:T(1,128)} %param.30) | copy-start | bytes 27652
  744.4 113.6 %copy-start.4 = (f32[1,14,128,128]{3,2,1,0:T(8,128)S(1)}, f32[1,14,128,128]{3,2,1,0:T(8,128)}, u32[]{:S(2)}) copy-start(f32[1,14,128,128]{3,2,1,0:T(8,128)} %param.26) | copy-start | bytes 2752516
  744.4 116.2 %copy-start.5 = (f32[1,14,128,128]{3,2,1,0:T(8,128)S(1)}, f32[1,14,128,128]{3,2,1,0:T(8,128)}, u32[]{:S(2)}) copy-start(f32[1,14,128,128]{3,2,1,0:T(8,128)} %param.25) | copy-start | bytes 2752516
  863.1 5.0 copy-start.6
  863.1 5.0 copy-start.7
  863.1 1.8 copy-start.1
  863.1 4.9 copy-start.3
  864.9 4.1 copy-start.2
Sparse Core Ops, SparseCore 0:
  11.4 108.1 all-gather.9
  222.1 43.0 all-gather.7
  266.8 44.9 all-gather.5
  696.4 161.6 reduce-scatter.1

commit v3 on v2

--- a/solution.py
+++ b/solution.py
@@ -1,3 +1,5 @@
+import functools
+
 import jax
 import jax.numpy as jnp
 from jax import lax
@@ -34,17 +36,6 @@
         D // block_edge * (ffn_width // block_edge),
         ffn_width // block_edge * (D // block_edge),
     )
-
-
-def rotate_update(gradient, moment_one, moment_two, left, right, master):
-    turned = jnp.einsum("psji,psjk->psik", left, gradient, precision=HIGHEST_PRECISION)
-    turned = jnp.einsum("psik,pskl->psil", turned, right, precision=HIGHEST_PRECISION)
-    first_new = MOMENT_DECAY * moment_one + (1.0 - MOMENT_DECAY) * turned
-    second_new = MOMENT_DECAY * moment_two + (1.0 - MOMENT_DECAY) * turned * turned
-    stepped = first_new / (jnp.sqrt(second_new) + EPS_ADAM)
-    turned_back = jnp.einsum("psij,psjk->psik", left, stepped, precision=HIGHEST_PRECISION)
-    turned_back = jnp.einsum("psik,pslk->psil", turned_back, right, precision=HIGHEST_PRECISION)
-    return (master - LEARN_RATE * turned_back, first_new, second_new)
 
 
 def adam_vector(gradient, moment_one, moment_two, current):
@@ -360,22 +351,6 @@
     at = store(dot_tn(get_blocks(nl_ref), get_blocks(up_ref)), at)
     at = store(dot_tn(x_ref[...], get_blocks(merged_ref)), at)
     at = store(dot_tn(att_ref[0], get_blocks(al_ref)), at)
-
-
-def slot_kernel(places, g_ref, zero_ref, out_ref, sem):
-    def step(s, carry):
-        @pl.when(places[s] >= 0)
-        def _():
-            pltpu.make_async_copy(g_ref.at[jnp.maximum(places[s], 0)], out_ref.at[s], sem).start()
-
-        @pl.when(places[s] < 0)
-        def _():
-            pltpu.make_async_copy(zero_ref.at[0], out_ref.at[s], sem).start()
-
-        return carry
-
-    lax.fori_loop(0, places.shape[0], step, 0)
-    pltpu.make_async_copy(out_ref, out_ref, sem).wait()
 
 
 def smem():
@@ -498,6 +473,313 @@
     return layer_own, input_own, grads, row_grad, up_grad, split_grad
 
 
+def bit_orders(n_dp, spd):
+    dp_bits = list(range(1, n_dp.bit_length() - 1))
+    near, far = dp_bits[:1], dp_bits[1:]
+    third = spd * 4 // 14
+    first = (spd - third) // 2
+    counts = (first, spd - third - first, third)
+    orders = ([-1] + near + far, near + [-1] + far, far + [-1] + near)
+    parts, at = [], 0
+    for order, count in zip(orders, counts):
+        if count:
+            parts.append((order, at, count))
+        at += count
+    return parts
+
+
+def bit_of(number, bit):
+    return number // (1 << bit) % 2
+
+
+def across(bit):
+    if bit < 0:
+        return {"tensor": 1 - lax.axis_index("tensor")}
+    me = lax.axis_index("dp")
+    return {"dp": me + (1 - 2 * bit_of(me, bit)) * (1 << bit)}
+
+
+def first_slot(order, code, core, n_dp, spd):
+    dp, tensor = lax.axis_index("dp"), lax.axis_index("tensor")
+    place = len(order) - 1
+    dev = core
+    for bit in order:
+        flip = bit_of(code, place)
+        mine = tensor if bit < 0 else bit_of(dp, bit)
+        dev = dev + (mine + flip) % 2 * (n_dp if bit < 0 else 1 << bit)
+        place -= 1
+    return dev * spd
+
+
+def greet(bits):
+    barrier = pltpu.get_barrier_semaphore()
+    for bit in bits:
+        pl.semaphore_signal(barrier, inc=1, device_id=across(bit), device_id_type=pl.DeviceIdType.MESH)
+    pl.semaphore_wait(barrier, len(bits))
+
+
+def remote(source, target, send, recv, bit):
+    return pltpu.make_async_remote_copy(
+        src_ref=source, dst_ref=target, send_sem=send, recv_sem=recv,
+        device_id=across(bit), device_id_type=pl.DeviceIdType.MESH,
+    )
+
+
+def gather_kernel(n_dp, spd, own_ref, vec_ref, all_ref, both_ref, local_sem, send_sem, recv_sem, core_send, core_recv, vec_send, vec_recv):
+    parts = bit_orders(n_dp, spd)
+    n_bits = len(parts[0][0])
+    core = bit_of(lax.axis_index("dp"), 0)
+    tensor = lax.axis_index("tensor")
+    greet([0] + parts[0][0])
+    mine = first_slot(parts[0][0], 0, core, n_dp, spd)
+    keep = pltpu.make_async_copy(own_ref, all_ref.at[pl.ds(mine, spd)], local_sem.at[0])
+    keep.start()
+    keep_vec = pltpu.make_async_copy(vec_ref, both_ref.at[pl.ds(tensor, 1)], local_sem.at[1])
+    keep_vec.start()
+    vec = remote(vec_ref, both_ref.at[pl.ds(tensor, 1)], vec_send, vec_recv, -1)
+    vec.start()
+
+    def piece(part, code, core_of):
+        order, at, count = part
+        return all_ref.at[pl.ds(first_slot(order, code, core_of, n_dp, spd) + at, count)]
+
+    def forward(p, code, level, source):
+        order = parts[p][0]
+        for stage in range(level, n_bits):
+            remote(
+                source, piece(parts[p], code, core), send_sem.at[p, stage, code],
+                recv_sem.at[p, code + (1 << stage)], order[n_bits - 1 - stage],
+            ).start()
+        remote(source, piece(parts[p], code, core), core_send.at[p, code], core_recv.at[p, code], 0).start()
+
+    for p, part in enumerate(parts):
+        forward(p, 0, 0, own_ref.at[pl.ds(part[1], part[2])])
+    for level in range(n_bits):
+        def arrive(j, carry):
+            code = (1 << level) + j
+            for p, part in enumerate(parts):
+                here = piece(part, code, core)
+                pltpu.make_async_copy(here, here, recv_sem.at[p, code]).wait()
+                forward(p, code, level + 1, here)
+            return carry
+
+        lax.fori_loop(0, 1 << level, arrive, 0)
+
+    def drain(code, carry):
+        for p, part in enumerate(parts):
+            here = piece(part, code, core)
+            there = piece(part, code, 1 - core)
+            pltpu.make_async_copy(here, here, core_send.at[p, code]).wait()
+            pltpu.make_async_copy(there, there, core_recv.at[p, code]).wait()
+        return carry
+
+    for stage in range(n_bits):
+        def sent(code, carry):
+            for p, part in enumerate(parts):
+                here = piece(part, code, core)
+                pltpu.make_async_copy(here, here, send_sem.at[p, stage, code]).wait()
+            return carry
+
+        lax.fori_loop(0, 1 << stage, sent, 0)
+    lax.fori_loop(0, 1 << n_bits, drain, 0)
+    keep.wait()
+    keep_vec.wait()
+    vec.wait()
+
+
+def gather_all(own, vec, n_dp, pieces, space):
+    spd, edge = own.shape[0], own.shape[-1]
+    parts = bit_orders(n_dp, spd)
+    n, n_bits = len(parts), len(parts[0][0])
+    dma = pltpu.SemaphoreType.DMA
+    return pl.pallas_call(
+        functools.partial(gather_kernel, n_dp, spd),
+        in_specs=[pl.BlockSpec(memory_space=pltpu.VMEM)] * 2,
+        out_specs=[pl.BlockSpec(memory_space=space), pl.BlockSpec(memory_space=pltpu.VMEM)],
+        out_shape=[
+            jax.ShapeDtypeStruct((pieces * n_dp * spd, edge, edge), BF16),
+            jax.ShapeDtypeStruct((pieces, vec.shape[1]), F32),
+        ],
+        scratch_shapes=[
+            dma((2,)), dma((n, n_bits, 1 << n_bits)), dma((n, 1 << n_bits)),
+            dma((n, 1 << n_bits)), dma((n, 1 << n_bits)), dma, dma,
+        ],
+        compiler_params=pltpu.CompilerParams(
+            vmem_limit_bytes=VMEM_LIMIT, collective_id=0, has_side_effects=True
+        ),
+        name="gather",
+    )(own, vec)
+
+
+def scatter_kernel(
+    n_dp, spd, scale, places, g_ref, vec_ref, out_ref, vec_out,
+    give_ref, sum_ref, in_ref, vec_sum, vec_in,
+    core_send, core_recv, send_sem, recv_sem, vec_send, vec_recv,
+):
+    parts = bit_orders(n_dp, spd)
+    n_bits = len(parts[0][0])
+    codes = 1 << n_bits
+    core = bit_of(lax.axis_index("dp"), 0)
+    vec_bits = [0] + parts[0][0]
+    greet(vec_bits)
+
+    def term(slot):
+        place = places[slot]
+        return jnp.where(place >= 0, g_ref[jnp.maximum(place, 0)], jnp.zeros(g_ref.shape[1:], BF16))
+
+    def vec_copy(stage):
+        return remote(vec_sum.at[stage], vec_in.at[stage], vec_send.at[stage], vec_recv.at[stage], vec_bits[stage])
+
+    def vec_step(stage):
+        vec_copy(stage).wait_recv()
+        total = vec_sum[stage] + vec_in[stage]
+        if stage + 1 < len(vec_bits):
+            vec_sum[stage + 1] = total
+            vec_copy(stage + 1).start()
+        else:
+            vec_out[...] = total * scale
+
+    vec_sum[0] = vec_ref[...]
+    vec_copy(0).start()
+
+    def give(p, code):
+        order, at, count = parts[p]
+        where = pl.ds(at, count)
+        return remote(
+            give_ref.at[code, where], sum_ref.at[code, where], core_send.at[p, code], core_recv.at[p, code], 0
+        )
+
+    def passed(p, level, code):
+        order, at, count = parts[p]
+        where = pl.ds(at, count)
+        return remote(
+            sum_ref.at[code, where], in_ref.at[code - 1, where],
+            send_sem.at[p, code], recv_sem.at[p, code - 1], order[n_bits - 1 - level],
+        )
+
+    def hand(j, carry):
+        code = codes - 1 - j
+        for p, (order, at, count) in enumerate(parts):
+            start = first_slot(order, code, 1 - core, n_dp, spd) + at
+            for s in range(count):
+                give_ref[code, at + s] = term(start + s)
+            give(p, code).start()
+        return carry
+
+    lax.fori_loop(0, codes, hand, 0)
+    vec_step(0)
+
+    def total_of(p, code, level, finish):
+        order, at, count = parts[p]
+        start = first_slot(order, code, core, n_dp, spd) + at
+        give(p, code).wait_recv()
+        sources = []
+        for stage in range(level + 1, n_bits):
+            entry = (1 << stage) - 1 + code
+            here = in_ref.at[entry, pl.ds(at, count)]
+            pltpu.make_async_copy(here, here, recv_sem.at[p, entry]).wait()
+            sources.append(entry)
+        for s in range(count):
+            value = term(start + s).astype(F32) + sum_ref[code, at + s].astype(F32)
+            for entry in sources:
+                value = value + in_ref[entry, at + s].astype(F32)
+            if finish:
+                out_ref[at + s] = value * scale
+            else:
+                sum_ref[code, at + s] = value.astype(BF16)
+
+    for level in reversed(range(n_bits)):
+        def onward(j, carry):
+            code = (2 << level) - 1 - j
+            for p in range(len(parts)):
+                total_of(p, code, level, False)
+                passed(p, level, code).start()
+            return carry
+
+        lax.fori_loop(0, 1 << level, onward, 0)
+        vec_step(n_bits - level)
+    for p in range(len(parts)):
+        total_of(p, 0, -1, True)
+    for stage in range(len(vec_bits)):
+        vec_copy(stage).wait_send()
+
+    def drain(code, carry):
+        for p in range(len(parts)):
+            give(p, code).wait_send()
+        return carry
+
+    lax.fori_loop(0, codes, drain, 0)
+    for level in range(n_bits):
+        def drain_level(j, carry):
+            for p in range(len(parts)):
+                passed(p, level, (1 << level) + j).wait_send()
+            return carry
+
+        lax.fori_loop(0, 1 << level, drain_level, 0)
+
+
+def scatter_all(places, grads, vec, n_dp, scale):
+    edge = grads.shape[-1]
+    spd = places.shape[0] // (2 * n_dp)
+    parts = bit_orders(n_dp, spd)
+    n, n_bits = len(parts), len(parts[0][0])
+    codes = 1 << n_bits
+    dma = pltpu.SemaphoreType.DMA
+    vmem = pl.BlockSpec(memory_space=pltpu.VMEM)
+    return pl.pallas_call(
+        functools.partial(scatter_kernel, n_dp, spd, scale),
+        in_specs=[smem(), vmem, vmem],
+        out_specs=[vmem, vmem],
+        out_shape=[
+            jax.ShapeDtypeStruct((spd, edge, edge), F32),
+            jax.ShapeDtypeStruct(vec.shape, F32),
+        ],
+        scratch_shapes=[
+            pltpu.VMEM((codes, spd, edge, edge), BF16),
+            pltpu.VMEM((codes, spd, edge, edge), BF16),
+            pltpu.VMEM((codes - 1, spd, edge, edge), BF16),
+            pltpu.VMEM((n_bits + 1,) + vec.shape, F32),
+            pltpu.VMEM((n_bits + 1,) + vec.shape, F32),
+            dma((n, codes)), dma((n, codes)), dma((n, codes)), dma((n, codes)),
+            dma((n_bits + 1,)), dma((n_bits + 1,)),
+        ],
+        compiler_params=pltpu.CompilerParams(
+            vmem_limit_bytes=VMEM_LIMIT, collective_id=1, has_side_effects=True
+        ),
+        name="scatter",
+    )(places, grads, vec)
+
+
+def update_kernel(grad_ref, master_ref, first_ref, second_ref, left_ref, right_ref, new_ref, nf_ref, ns_ref, low_ref):
+    for s in range(grad_ref.shape[0]):
+        left, right = left_ref[0, s].astype(BF16), right_ref[0, s].astype(BF16)
+        turned = dot_nn(dot_tn(left, grad_ref[s].astype(BF16)).astype(BF16), right)
+        first = MOMENT_DECAY * first_ref[0, s] + (1.0 - MOMENT_DECAY) * turned
+        second = MOMENT_DECAY * second_ref[0, s] + (1.0 - MOMENT_DECAY) * turned * turned
+        stepped = first / (jnp.sqrt(second) + EPS_ADAM)
+        back = dot_nt(dot_nn(left, stepped.astype(BF16)).astype(BF16), right)
+        new = master_ref[0, s] - LEARN_RATE * back
+        new_ref[0, s] = new
+        nf_ref[0, s] = first
+        ns_ref[0, s] = second
+        low_ref[0, s] = new.astype(BF16)
+
+
+def update_blocks(grads, masters, first, second, left, right):
+    spd, edge = grads.shape[0], grads.shape[-1]
+    group = 2 if spd % 2 == 0 else 1
+    spec = pl.BlockSpec((1, group, edge, edge), lambda i: (0, i, 0, 0))
+    return pl.pallas_call(
+        update_kernel,
+        grid=(spd // group,),
+        in_specs=[pl.BlockSpec((group, edge, edge), lambda i: (i, 0, 0))] + [spec] * 5,
+        out_specs=[spec] * 4,
+        out_shape=[jax.ShapeDtypeStruct(masters.shape, F32)] * 3 + [jax.ShapeDtypeStruct(masters.shape, BF16)],
+        compiler_params=params(),
+        name="update",
+    )(grads, masters, first, second, left, right)
+
+
 def body(
     tokens,
     cotangent,
@@ -524,11 +806,11 @@
     slots = block_of_slot.shape[0]
     full_seq = tokens.shape[0] // pair_lengths.shape[0]
     row_count = pair_lengths.shape[0] // pieces
-    every = lax.all_gather(masters[0].astype(BF16), ("tensor", "dp"), axis=0, tiled=True)
+    n_dp = lax.axis_size("dp")
+    every, split_all = gather_all(masters[0].astype(BF16), split_vec, n_dp, pieces, pl.ANY)
     slot_of = slot_table(block_of_slot, block_total)
     order = np.array(sum(block_home(pieces), []), np.int32)
     homes = slot_of[order[:, 1]] + order[:, 0] * slots
-    split_all = lax.all_gather(split_vec[0], "tensor", axis=0)
     query_bias = split_all[:, :piece_width].reshape(1, -1)
     value_bias = split_all[:, piece_width : 2 * piece_width].reshape(1, -1)
     up_bias = split_all[:, 2 * piece_width :].reshape(1, -1)
@@ -541,14 +823,6 @@
     for index, (at_piece, number) in enumerate(grad_order(pieces)):
         place_table[at_piece, number] = index
     places = jnp.asarray(place_table)[:, block_of_slot].reshape(-1)
-    slot_terms = pl.pallas_call(
-        slot_kernel,
-        in_specs=[smem(), anywhere(), anywhere()],
-        out_specs=anywhere(),
-        out_shape=jax.ShapeDtypeStruct((pieces * slots, block_edge, block_edge), BF16),
-        scratch_shapes=[pltpu.SemaphoreType.DMA],
-        name="slots",
-    )(places, grads, jnp.zeros((1, block_edge, block_edge), BF16))
     split_local = jnp.concatenate(
         [
             qv_grad[0].reshape(pieces, piece_width),
@@ -557,17 +831,15 @@
         ],
         axis=1,
     )
-    token_total = tokens.shape[0] * lax.axis_size("dp")
-    mean_scale = 1.0 / token_total
-    owned_sum = lax.psum_scatter(
-        slot_terms, ("tensor", "dp"), scatter_dimension=0, tiled=True
-    ).astype(F32)
-    split_total, row_total = lax.psum((split_local, row_local), ("tensor", "dp"))
-    weight_grads = (owned_sum * mean_scale)[None]
-    split_grad = lax.dynamic_slice_in_dim(split_total, piece, 1, 0) * mean_scale
-    row_grad = row_total * mean_scale
-    new_masters, new_first, new_second = rotate_update(
-        weight_grads, mom_first, mom_second, left_bases, right_bases, masters
+    mean_scale = 1.0 / (tokens.shape[0] * n_dp)
+    vectors = jnp.concatenate([split_local.reshape(-1, LANES), row_local.reshape(-1, LANES)], axis=0)
+    owned, summed = scatter_all(places, grads, vectors, n_dp, mean_scale)
+    weight_grads = owned[None]
+    split_rows = split_local.size // LANES
+    split_grad = lax.dynamic_slice_in_dim(summed[:split_rows].reshape(pieces, -1), piece, 1, 0)
+    row_grad = summed[split_rows:].reshape(row_local.shape)
+    new_masters, new_first, new_second, copies = update_blocks(
+        owned, masters, mom_first, mom_second, left_bases, right_bases
     )
     new_split, new_split_first, new_split_second = adam_vector(
         split_grad, split_first, split_second, split_vec
@@ -580,7 +852,7 @@
         new_masters,
         new_first,
         new_second,
-        new_masters.astype(jnp.bfloat16),
+        copies,
         split_grad,
         new_split,
         new_split_first,

time: 878 us -> 343 us (0.39)
  Pallas kernels: 573 us -> 300 us
  waiting for transfers between devices: 207 us -> 0.71 us
  blocking collectives: 50.5 us -> 0 us
  matrix products: 9.45 us -> 0 us
    pallas_call x1 -> x3, Pallas kernels: 447 us -> 174 us  [the longest x1 96.5 us: scatter_all(): pl.pallas_call(functools.partial(scatter_kernel, n_dp, spd, scale), in_sp...]
    reduce_scatter x1 -> x0, waiting for transfers between devices: 108 us -> none  [body(): lax.psum_scatter(slot_terms, ('tensor', 'dp'), scatter_dimension=0, tiled...]
    all_gather x1 -> x0, waiting for transfers between devices: 97.6 us -> none  [body(): lax.all_gather(masters[0].astype(BF16), ('tensor', 'dp'), axis=0, tiled=T...]
    psum x1 -> x0, blocking collectives: 45 us -> none  [body(): lax.psum((split_local, row_local), ('tensor', 'dp'))]
    dot_general x4 -> x0, matrix products: 9.45 us -> none  [the longest x1 3.1 us: rotate_update(): jnp.einsum('psik,pslk->psil', turned_back, right, precision=HIGHEST_PRECI...]
  transfers between devices with their start and end apart: 4 -> 2, of which waited for: 2 -> 0; matrix products, arithmetic and copies ran while one was open for 2% -> 3% of each run, Pallas kernels for 54% -> 38%
where the time goes in v3:
time: 343 us; the launch traced here: 342 us
  Pallas kernels  300 us (87%)
  local copies, waits for them, and re-layouts  14.9 us (4%)
  between operations  14.3 us (4%)
  other arithmetic  11.8 us (3%)
    pallas_call x1, Pallas kernels, scatter_all(): pl.pallas_call(functools.partial(scatter_kernel, n_dp, spd, scale), in_sp...  96.5 us
    pallas_call x1, Pallas kernels, gather_all(): pl.pallas_call(functools.partial(gather_kernel, n_dp, spd), in_specs=[pl....  67.9 us
    pallas_call x1, Pallas kernels, layer_passes(): pl.pallas_call(lambda homes, off, *refs: token_kernel(homes, *refs), grid...  48.2 us
    pallas_call x1, Pallas kernels, layer_passes(): pl.pallas_call(attend_back_kernel, grid_spec=pltpu.PrefetchScalarGridSpec...  29.5 us
    pallas_call x1, Pallas kernels, layer_passes(): pl.pallas_call(attend_kernel, grid_spec=pltpu.PrefetchScalarGridSpec(num_...  24.6 us
    pallas_call x1, Pallas kernels, layer_passes(): pl.pallas_call(lambda pc, *refs: grad_kernel(*refs), grid_spec=pltpu.Pref...  23.9 us
    pallas_call x1, Pallas kernels, update_blocks(): pl.pallas_call(update_kernel, grid=(spd // group,), in_specs=[pl.BlockSpe...  9.31 us
    unnamed x33, local copies, waits for them, and re-layouts  8.01 us
  transfers between devices with their start and end apart: 2, of which 0 were waited for; matrix products, arithmetic and copies ran while one was open for 3% of the time, Pallas kernels for 38%

profile of v3, /device:TPU:0, one launch (start us, length us, event | category | flops | bytes accessed | tf_op | source)
XLA Modules:
  0.0 341.8 jit_solution(16798478387846502932)
XLA Ops:
  7.2 0.0 all-gather.5.cloned.1.call-start
  7.2 2.0 convert_bitcast_fusion.own_ref
  9.3 67.9 %gather.13 = (bf16[448,128,128]{2,1,0:T(8,128)(2,1)}, f32[2,2304]{1,0:T(2,128)}) custom-call(bf16[14,128,128]{2,1,0:T(8,128)(2,1)} %convert_bitcast_fusion.own_ref, f32[1,2304]{1,0:T(1,128)} %vec_ref.1), custom_call_target="tpu_custom_call" | custom-call | tf_op jit(solution)/shard_map/gather/pallas_call | solution.py:595
  77.2 0.7 slice_bitcast_fusion.1
  77.9 0.7 slice_bitcast_fusion
  78.6 0.6 copy.37
  79.2 0.6 copy.36
  79.8 0.7 pad_clamp_fusion.1
  80.5 0.8 select_reduce_fusion
  81.3 0.6 copy.38
  81.9 3.1 gather_fusion
  85.0 0.6 add.44.homes
  85.6 24.6 %attend.1 = (bf16[18,1024,128]{2,1,0:T(8,128)(2,1)}, bf16[6,1024,128]{2,1,0:T(8,128)(2,1)}, f32[2,12,1,512]{3,2,1,0:T(1,128)}) custom-call(s32[432]{0:T(512)} %add.44.homes, s32[4,4]{1,0:T(4,128)} %pairs.3, s32[1]{0:T(128)} %bitcast.offset.off, bf16[2048,768]{1,0:T(8,128)(2,1)} %refs_4_.1, bf16[448,128,128]{2,1,0:T(8,128)(2,1)} %get-tuple-element.39.every.refs_3_, ...), custom_call_target="tpu_custom_call" | custom-call | tf_op jit(solution)/shard_map/attend/pallas_call | solution.py:378
  110.3 48.2 %tokenwise.1 = (bf16[1024,768]{1,0:T(8,128)(2,1)}, bf16[6,1024,128]{2,1,0:T(8,128)(2,1)}, bf16[24,1024,128]{2,1,0:T(8,128)(2,1)}, bf16[6,1024,128]{2,1,0:T(8,128...) custom-call(s32[432]{0:T(512)} %add.44.homes, ...), custom_call_target="tpu_custom_call" | custom-call | tf_op jit(solution)/shard_map/tokenwise/pallas_call | solution.py:399
  158.4 29.5 %attend_back.1 = (bf16[18,1024,128]{2,1,0:T(8,128)(2,1)}, bf16[1024,768]{1,0:T(8,128)(2,1)}, f32[2,768]{1,0:T(2,128)}) custom-call(s32[432]{0:T(512)} %add.44.homes, s32[4,4]{1,0:T(4,128)} %pairs.3, s32[1]{0:T(128)} %bitcast.offset.off, bf16[18,1024,128]{2,1,0:T(8,128)(2,1)} %get-tuple-element.43.qkv_ref, ...), custom_call_target="tpu_custom_call" | custom-call | tf_op jit(solution)/shard_map/attend_back/pallas_call | solution.py:433
  188.1 0.0 all-gather.3.cloned.1.call-start
  188.1 0.7 all-gather.3.cloned.1.call-update
  188.9 0.5 broadcast.26
  189.4 0.7 reduce.7
  190.2 1.6 gather_fusion.1
  191.8 0.1 copy.35
  191.9 0.7 reshape.69.places
  192.5 23.9 %weight_grads.1.g_ref = bf16[432,128,128]{2,1,0:T(8,128)(2,1)} custom-call(s32[1]{0:T(128)} %bitcast.3.pc, bf16[24,1024,128]{2,1,0:T(8,128)(2,1)} %get-tuple-element.48.refs_0_, bf16[6,1024,128]{2,1,0:T(8,128)(2,1)} %get-tuple-element.49.refs_1_, bf16[6,1024,128]{2,1,0:T(8,128)(2,1)} %get-tuple-element.50.refs_2_, ...), custom_call_target="tpu_custom_call" | custom-call | tf_op jit(solution)/shard_map/weight_grads/pallas_call | solution.py:457
  216.4 0.6 pad_maximum_fusion.vec_ref
  217.0 96.5 %scatter.1 = (f32[14,128,128]{2,1,0:T(8,128)}, f32[72,128]{1,0:T(8,128)}) custom-call(s32[448]{0:T(512)} %reshape.69.places, bf16[432,128,128]{2,1,0:T(8,128)(2,1)} %weight_grads.1.g_ref, f32[72,128]{1,0:T(8,128)} %pad_maximum_fusion.vec_ref), custom_call_target="tpu_custom_call" | custom-call | tf_op jit(solution)/shard_map/scatter/pallas_call | solution.py:729
  313.7 0.8 fusion.4
  314.5 9.3 %update.1 = (f32[1,14,128,128]{3,2,1,0:T(8,128)}, f32[1,14,128,128]{3,2,1,0:T(8,128)}, f32[1,14,128,128]{3,2,1,0:T(8,128)}, bf16[1,14,128,128]{3,2,1,0:T(8,128)(2,1)}) custom-call(f32[14,128,128]{2,1,0:T(8,128)} %get-tuple-element.57.grad_ref, f32[1,14,128,128]{3,2,1,0:T(8,128)} %master_ref.1, f32[1,14,128,128]{3,2,1,0:T(8,128)} %first_ref.1, ...), custom_call_target="tpu_custom_call" | custom-call | tf_op jit(solution)/shard_map/update/pallas_call | solution.py:772
  323.8 0.6 divide_subtract_fusion
  324.5 0.7 divide_subtract_fusion.1
  325.2 5.1 %convert_element_type.10 = f32[2048,768]{1,0:T(8,128)} convert(bf16[2048,768]{1,0:T(8,128)(2,1)} %all-gather.5.cloned.1.call-done) | non-fusion elementwise | flops 1572864 | bytes 9437184 | tf_op jit(solution)/shard_map/convert_element_type | solution.py:821
  330.2 3.8 %copy.41 = bf16[2048,768]{1,0:T(8,128)(2,1)} copy(bf16[2048,768]{1,0:T(8,128)(2,1)} %all-gather.3.cloned.1.call-done) | data formatting | bytes 6291456
  334.1 0.9 copy.42
  (40 shorter events, 0.2 us)
Async XLA Ops:
  7.2 77.9 %copy-start.12 = (s32[432]{0:T(512)S(1)}, s32[432]{0:T(512)}, u32[]{:S(2)}) copy-start(s32[432]{0:T(512)} %constant.10.clone) | copy-start | bytes 5188
  7.2 318.0 %all-gather.5.cloned.1.call-start = ((), (), s32[]{:S(2)}) async-start(), calls=%async_computation.1 | async-start | bytes 4718592 | tf_op jit(solution)/shard_map/all_gather | solution.py:821
  188.0 0.8 copy-start.10
  188.0 1.4 copy-start.7
  188.0 2.1 copy-start.4
  188.0 2.1 copy-start.11
  188.1 142.2 %all-gather.3.cloned.1.call-start = ((), (), s32[]{:S(2)}) async-start(), calls=%async_computation | async-start | bytes 4718592 | tf_op jit(solution)/shard_map/all_gather | solution.py:820
  313.6 10.2 %copy-start.1 = (f32[6,768]{1,0:T(8,128)S(1)}, f32[6,768]{1,0:T(8,128)}, u32[]{:S(2)}) copy-start(f32[6,768]{1,0:T(8,128)} %refs_5_.1) | copy-start | bytes 55300
  313.6 10.2 %copy-start.5 = (f32[6,768]{1,0:T(8,128)S(1)}, f32[6,768]{1,0:T(8,128)}, u32[]{:S(2)}) copy-start(f32[6,768]{1,0:T(8,128)} %param.32) | copy-start | bytes 55300
  313.6 10.2 %copy-start.6 = (f32[6,768]{1,0:T(8,128)S(1)}, f32[6,768]{1,0:T(8,128)}, u32[]{:S(2)}) copy-start(f32[6,768]{1,0:T(8,128)} %param.33) | copy-start | bytes 55300
  313.6 10.9 %copy-start.3 = (f32[1,2304]{1,0:T(1,128)S(1)}, f32[1,2304]{1,0:T(1,128)}, u32[]{:S(2)}) copy-start(f32[1,2304]{1,0:T(1,128)} %vec_ref.1) | copy-start | bytes 27652
  313.6 10.8 %copy-start.8 = (f32[1,2304]{1,0:T(1,128)S(1)}, f32[1,2304]{1,0:T(1,128)}, u32[]{:S(2)}) copy-start(f32[1,2304]{1,0:T(1,128)} %param.29) | copy-start | bytes 27652
  313.6 10.8 %copy-start.9 = (f32[1,2304]{1,0:T(1,128)S(1)}, f32[1,2304]{1,0:T(1,128)}, u32[]{:S(2)}) copy-start(f32[1,2304]{1,0:T(1,128)} %param.30) | copy-start | bytes 27652
  314.5 15.8 %copy-start.2 = (f32[6,768]{1,0:T(8,128)}, f32[6,768]{1,0:T(8,128)S(1)}, u32[]{:S(2)}) copy-start(f32[6,768]{1,0:T(8,128)S(1)} %reshape.75) | copy-start | bytes 55300
  330.2 3.8 %copy-start = (f32[14,128,128]{2,1,0:T(8,128)S(1)}, f32[14,128,128]{2,1,0:T(8,128)}, u32[]{:S(2)}) copy-start(f32[14,128,128]{2,1,0:T(8,128)} %get-tuple-element.57.grad_ref) | copy-start | bytes 2752516
Sparse Core Ops, SparseCore 0:
  188.2 45.9 all-gather.4
  235.7 77.8 all-gather.2

commit v4 on v3

--- a/solution.py
+++ b/solution.py
@@ -23,28 +23,12 @@
 HIGHEST_PRECISION = lax.Precision.HIGHEST
 
 
-def slot_table(block_of_slot, block_total):
-    slot_numbers = jnp.arange(block_of_slot.shape[0], dtype=jnp.int32)
-    matches = block_of_slot[:, None] == jnp.arange(block_total, dtype=jnp.int32)[None, :]
-    return jnp.sum(jnp.where(matches, slot_numbers[:, None], 0), axis=0)
-
-
 def block_counts(block_edge, head_width, ffn_width):
     return (
         D // block_edge * (3 * head_width // block_edge),
         head_width // block_edge * (D // block_edge),
         D // block_edge * (ffn_width // block_edge),
         ffn_width // block_edge * (D // block_edge),
-    )
-
-
-def adam_vector(gradient, moment_one, moment_two, current):
-    first_new = MOMENT_DECAY * moment_one + (1.0 - MOMENT_DECAY) * gradient
-    second_new = MOMENT_DECAY * moment_two + (1.0 - MOMENT_DECAY) * gradient * gradient
-    return (
-        current - VECTOR_RATE * first_new / (jnp.sqrt(second_new) + EPS_ADAM),
-        first_new,
-        second_new,
     )
 
 
@@ -56,6 +40,7 @@
 ERF_A = (0.254829592, -0.284496736, 1.421413741, -1.453152027, 1.061405429)
 VMEM_LIMIT = 60 * 1024 * 1024
 LANES = 128
+VEC_ROWS = 16
 BF16 = jnp.bfloat16
 F32 = jnp.float32
 
@@ -280,7 +265,7 @@
 
 def attend_back_kernel(
     homes, pairs, offset, qkv_ref, att_ref, ml_ref, lse_ref, g1_ref, every,
-    merged_ref, ig_ref, sg_ref, w_ref, bias_ref, sem,
+    merged_ref, ig_ref, il_ref, sg_ref, w_ref, bias_ref, sem,
 ):
     d_b = D // LANES
     row = pl.program_id(0)
@@ -331,7 +316,9 @@
         sg_ref[0:1, at] += jnp.sum(merged_ref[n].astype(F32), axis=0, keepdims=True)
         sg_ref[1:2, at] += jnp.sum(merged_ref[2 * d_b + n].astype(F32), axis=0, keepdims=True)
     merged = get_blocks(merged_ref)
-    ig_ref[...] = (g1_ref[...] + dot_nt(merged, w_ref[...])).astype(BF16)
+    total = g1_ref[...] + dot_nt(merged, w_ref[...])
+    ig_ref[...] = total
+    il_ref[...] = total.astype(BF16)
 
 
 def grad_kernel(act_ref, dl_ref, nl_ref, up_ref, x_ref, merged_ref, att_ref, al_ref, g_ref):
@@ -394,6 +381,7 @@
             shape((row_count, HEADS, 1, seq), F32),
         ],
         compiler_params=params(),
+        cost_estimate=pl.CostEstimate(flops=24 * total * D * D, bytes_accessed=32 * total * D, transcendentals=0),
         name="attend",
     )(homes, pair_lengths, offset, tokens, every, query_bias, value_bias)
     token_outs = pl.pallas_call(
@@ -427,16 +415,19 @@
             shape((1, FF), F32),
         ],
         compiler_params=params(),
+        cost_estimate=pl.CostEstimate(flops=40 * total * D * D, bytes_accessed=64 * total * D, transcendentals=0),
         name="tokenwise",
     )(homes, offset, att, tokens, cotangent, every, up_bias, row_vec)
     layer_own, normed_low, active_low, down_low, up_low, attn_low, mixed_low, grad_one, row_grad, up_grad = token_outs
-    merged, input_own, split_grad = pl.pallas_call(
+    swap = [(0, 1), (1, 0)]
+    layer_other = lax.ppermute(layer_own, "tensor", swap)
+    merged, input_own, input_low, split_grad = pl.pallas_call(
         attend_back_kernel,
         grid_spec=pltpu.PrefetchScalarGridSpec(
             num_scalar_prefetch=3,
             grid=(row_count,),
             in_specs=[stack(3 * d_b), stack(d_b), stack(d_b), lse_spec, rows, anywhere()],
-            out_specs=[stack(3 * d_b), rows, whole((2, D))],
+            out_specs=[stack(3 * d_b), rows, rows, whole((2, D))],
             scratch_shapes=[
                 pltpu.VMEM((D, 3 * D), BF16),
                 pltpu.VMEM((seq, seq), F32),
@@ -445,12 +436,15 @@
         ),
         out_shape=[
             shape((3 * d_b, total, LANES), BF16),
+            shape((total, D), F32),
             shape((total, D), BF16),
             shape((2, D), F32),
         ],
         compiler_params=params(),
+        cost_estimate=pl.CostEstimate(flops=32 * total * D * D, bytes_accessed=40 * total * D, transcendentals=0),
         name="attend_back",
     )(homes, pair_lengths, offset, qkv, att, mixed_low, lse, grad_one, every)
+    input_other = lax.ppermute(input_low, "tensor", swap)
     f_s = f_b // d_b
     part = lambda n: pl.BlockSpec((n, total, LANES), lambda j, *_: (j, 0, 0))
     blocks = 2 * f_s * d_b + 4 * d_b
@@ -468,9 +462,10 @@
         ),
         out_shape=shape((d_b * blocks, LANES, LANES), BF16),
         compiler_params=params(),
+        cost_estimate=pl.CostEstimate(flops=24 * total * D * D, bytes_accessed=40 * total * D, transcendentals=0),
         name="weight_grads",
     )(piece.astype(jnp.int32).reshape(1), active_low, down_low, normed_low, up_low, tokens, merged, att, attn_low)
-    return layer_own, input_own, grads, row_grad, up_grad, split_grad
+    return layer_own, layer_other, input_own, input_other, grads, row_grad, up_grad, split_grad
 
 
 def bit_orders(n_dp, spd):
@@ -499,16 +494,28 @@
     return {"dp": me + (1 - 2 * bit_of(me, bit)) * (1 << bit)}
 
 
-def first_slot(order, code, core, n_dp, spd):
+def place_of(order, code, core):
     dp, tensor = lax.axis_index("dp"), lax.axis_index("tensor")
     place = len(order) - 1
-    dev = core
+    to_dp, to_tensor = core, tensor
     for bit in order:
         flip = bit_of(code, place)
-        mine = tensor if bit < 0 else bit_of(dp, bit)
-        dev = dev + (mine + flip) % 2 * (n_dp if bit < 0 else 1 << bit)
+        if bit < 0:
+            to_tensor = (tensor + flip) % 2
+        else:
+            to_dp = to_dp + (bit_of(dp, bit) + flip) % 2 * (1 << bit)
         place -= 1
-    return dev * spd
+    return to_tensor, to_dp
+
+
+def slot_at(order, code, core, spd, at):
+    to_tensor, to_dp = place_of(order, code, core)
+    return to_tensor, to_dp * spd + at
+
+
+def first_slot(order, code, core, n_dp, spd):
+    to_tensor, to_dp = place_of(order, code, core)
+    return (to_tensor * n_dp + to_dp) * spd
 
 
 def greet(bits):
@@ -525,12 +532,13 @@
     )
 
 
-def gather_kernel(n_dp, spd, own_ref, vec_ref, all_ref, both_ref, local_sem, send_sem, recv_sem, core_send, core_recv, vec_send, vec_recv):
+def gather_kernel(n_dp, spd, master_ref, vec_ref, all_ref, qb_ref, vb_ref, bu_ref, own_ref, both_ref, local_sem, send_sem, recv_sem, core_send, core_recv, vec_send, vec_recv):
     parts = bit_orders(n_dp, spd)
     n_bits = len(parts[0][0])
     core = bit_of(lax.axis_index("dp"), 0)
     tensor = lax.axis_index("tensor")
     greet([0] + parts[0][0])
+    own_ref[...] = master_ref[0].astype(BF16)
     mine = first_slot(parts[0][0], 0, core, n_dp, spd)
     keep = pltpu.make_async_copy(own_ref, all_ref.at[pl.ds(mine, spd)], local_sem.at[0])
     keep.start()
@@ -573,6 +581,15 @@
             pltpu.make_async_copy(there, there, core_recv.at[p, code]).wait()
         return carry
 
+    keep_vec.wait()
+    vec.wait()
+    pieces = both_ref.shape[0]
+    head_w, ffn_w = D // pieces, FF // pieces
+    for i in range(pieces):
+        row = both_ref[i : i + 1]
+        qb_ref[:, i * head_w : (i + 1) * head_w] = row[:, :head_w]
+        vb_ref[:, i * head_w : (i + 1) * head_w] = row[:, head_w : 2 * head_w]
+        bu_ref[:, i * ffn_w : (i + 1) * ffn_w] = row[:, 2 * head_w :]
     for stage in range(n_bits):
         def sent(code, carry):
             for p, part in enumerate(parts):
@@ -583,24 +600,26 @@
         lax.fori_loop(0, 1 << stage, sent, 0)
     lax.fori_loop(0, 1 << n_bits, drain, 0)
     keep.wait()
-    keep_vec.wait()
-    vec.wait()
-
-
-def gather_all(own, vec, n_dp, pieces, space):
-    spd, edge = own.shape[0], own.shape[-1]
+
+
+def gather_all(masters, vec, n_dp, pieces):
+    spd, edge = masters.shape[1], masters.shape[-1]
     parts = bit_orders(n_dp, spd)
     n, n_bits = len(parts), len(parts[0][0])
     dma = pltpu.SemaphoreType.DMA
+    vmem = pl.BlockSpec(memory_space=pltpu.VMEM)
+    shape = jax.ShapeDtypeStruct
     return pl.pallas_call(
         functools.partial(gather_kernel, n_dp, spd),
-        in_specs=[pl.BlockSpec(memory_space=pltpu.VMEM)] * 2,
-        out_specs=[pl.BlockSpec(memory_space=space), pl.BlockSpec(memory_space=pltpu.VMEM)],
+        in_specs=[vmem] * 2,
+        out_specs=[anywhere()] + [vmem] * 3,
         out_shape=[
-            jax.ShapeDtypeStruct((pieces * n_dp * spd, edge, edge), BF16),
-            jax.ShapeDtypeStruct((pieces, vec.shape[1]), F32),
+            shape((pieces * n_dp * spd, edge, edge), BF16),
+            shape((1, D), F32), shape((1, D), F32), shape((1, FF), F32),
         ],
         scratch_shapes=[
+            pltpu.VMEM((spd, edge, edge), BF16),
+            pltpu.VMEM((pieces, vec.shape[1]), F32),
             dma((2,)), dma((n, n_bits, 1 << n_bits)), dma((n, 1 << n_bits)),
             dma((n, 1 << n_bits)), dma((n, 1 << n_bits)), dma, dma,
         ],
@@ -608,11 +627,11 @@
             vmem_limit_bytes=VMEM_LIMIT, collective_id=0, has_side_effects=True
         ),
         name="gather",
-    )(own, vec)
+    )(masters, vec)
 
 
 def scatter_kernel(
-    n_dp, spd, scale, places, g_ref, vec_ref, out_ref, vec_out,
+    n_dp, spd, scale, places, g_ref, rg_ref, sg_ref, bg_ref, out_ref, vec_out,
     give_ref, sum_ref, in_ref, vec_sum, vec_in,
     core_send, core_recv, send_sem, recv_sem, vec_send, vec_recv,
 ):
@@ -624,7 +643,7 @@
     greet(vec_bits)
 
     def term(slot):
-        place = places[slot]
+        place = places[slot[0], slot[1]]
         return jnp.where(place >= 0, g_ref[jnp.maximum(place, 0)], jnp.zeros(g_ref.shape[1:], BF16))
 
     def vec_copy(stage):
@@ -639,7 +658,11 @@
         else:
             vec_out[...] = total * scale
 
-    vec_sum[0] = vec_ref[...]
+    vec_sum[0, 0:6] = rg_ref[...]
+    vec_sum[0, 6:8] = sg_ref[...]
+    for i in range(FF // D):
+        vec_sum[0, 8 + i : 9 + i] = bg_ref[:, i * D : (i + 1) * D]
+    vec_sum[0, 8 + FF // D :] = jnp.zeros((VEC_ROWS - 8 - FF // D, D), F32)
     vec_copy(0).start()
 
     def give(p, code):
@@ -657,21 +680,23 @@
             send_sem.at[p, code], recv_sem.at[p, code - 1], order[n_bits - 1 - level],
         )
 
-    def hand(j, carry):
-        code = codes - 1 - j
+    def hand(code):
         for p, (order, at, count) in enumerate(parts):
-            start = first_slot(order, code, 1 - core, n_dp, spd) + at
+            start = slot_at(order, code, 1 - core, spd, at)
             for s in range(count):
-                give_ref[code, at + s] = term(start + s)
+                give_ref[code, at + s] = term((start[0], start[1] + s))
             give(p, code).start()
+
+    ahead = min(4, codes)
+    def first_hands(j, carry):
+        hand(codes - 1 - j)
         return carry
 
-    lax.fori_loop(0, codes, hand, 0)
-    vec_step(0)
+    lax.fori_loop(0, ahead, first_hands, 0)
 
     def total_of(p, code, level, finish):
         order, at, count = parts[p]
-        start = first_slot(order, code, core, n_dp, spd) + at
+        start = slot_at(order, code, core, spd, at)
         give(p, code).wait_recv()
         sources = []
         for stage in range(level + 1, n_bits):
@@ -680,7 +705,7 @@
             pltpu.make_async_copy(here, here, recv_sem.at[p, entry]).wait()
             sources.append(entry)
         for s in range(count):
-            value = term(start + s).astype(F32) + sum_ref[code, at + s].astype(F32)
+            value = term((start[0], start[1] + s)).astype(F32) + sum_ref[code, at + s].astype(F32)
             for entry in sources:
                 value = value + in_ref[entry, at + s].astype(F32)
             if finish:
@@ -691,15 +716,18 @@
     for level in reversed(range(n_bits)):
         def onward(j, carry):
             code = (2 << level) - 1 - j
+            if (1 << level) >= ahead:
+                hand(code - ahead)
             for p in range(len(parts)):
                 total_of(p, code, level, False)
                 passed(p, level, code).start()
             return carry
 
         lax.fori_loop(0, 1 << level, onward, 0)
-        vec_step(n_bits - level)
+        vec_step(n_bits - 1 - level)
     for p in range(len(parts)):
         total_of(p, 0, -1, True)
+    vec_step(n_bits)
     for stage in range(len(vec_bits)):
         vec_copy(stage).wait_send()
 
@@ -718,9 +746,9 @@
         lax.fori_loop(0, 1 << level, drain_level, 0)
 
 
-def scatter_all(places, grads, vec, n_dp, scale):
+def scatter_all(places, grads, row_grad, qv_grad, up_grad, n_dp, scale):
     edge = grads.shape[-1]
-    spd = places.shape[0] // (2 * n_dp)
+    spd = places.shape[1] // n_dp
     parts = bit_orders(n_dp, spd)
     n, n_bits = len(parts), len(parts[0][0])
     codes = 1 << n_bits
@@ -728,18 +756,18 @@
     vmem = pl.BlockSpec(memory_space=pltpu.VMEM)
     return pl.pallas_call(
         functools.partial(scatter_kernel, n_dp, spd, scale),
-        in_specs=[smem(), vmem, vmem],
+        in_specs=[smem()] + [vmem] * 4,
         out_specs=[vmem, vmem],
         out_shape=[
             jax.ShapeDtypeStruct((spd, edge, edge), F32),
-            jax.ShapeDtypeStruct(vec.shape, F32),
+            jax.ShapeDtypeStruct((VEC_ROWS, D), F32),
         ],
         scratch_shapes=[
             pltpu.VMEM((codes, spd, edge, edge), BF16),
             pltpu.VMEM((codes, spd, edge, edge), BF16),
             pltpu.VMEM((codes - 1, spd, edge, edge), BF16),
-            pltpu.VMEM((n_bits + 1,) + vec.shape, F32),
-            pltpu.VMEM((n_bits + 1,) + vec.shape, F32),
+            pltpu.VMEM((n_bits + 1, VEC_ROWS, D), F32),
+            pltpu.VMEM((n_bits + 1, VEC_ROWS, D), F32),
             dma((n, codes)), dma((n, codes)), dma((n, codes)), dma((n, codes)),
             dma((n_bits + 1,)), dma((n_bits + 1,)),
         ],
@@ -747,37 +775,93 @@
             vmem_limit_bytes=VMEM_LIMIT, collective_id=1, has_side_effects=True
         ),
         name="scatter",
-    )(places, grads, vec)
-
-
-def update_kernel(grad_ref, master_ref, first_ref, second_ref, left_ref, right_ref, new_ref, nf_ref, ns_ref, low_ref):
+    )(places, grads, row_grad, qv_grad, up_grad)
+
+
+def adam(grad, first, second, current, outs):
+    first = MOMENT_DECAY * first + (1.0 - MOMENT_DECAY) * grad
+    second = MOMENT_DECAY * second + (1.0 - MOMENT_DECAY) * grad * grad
+    grad_out, new_out, first_out, second_out = outs
+    grad_out[...] = grad
+    new_out[...] = current - VECTOR_RATE * first / (jnp.sqrt(second) + EPS_ADAM)
+    first_out[...] = first
+    second_out[...] = second
+
+
+def update_kernel(
+    piece, grad_ref, master_ref, first_ref, second_ref, left_ref, right_ref,
+    layer_own, layer_other, input_own, input_other, vec_ref, split_ref, sf_ref, ss_ref, row_ref, rf_ref, rs_ref,
+    wg_ref, new_ref, nf_ref, ns_ref, low_ref, layer_ref, input_ref, *vec_outs,
+):
+    step = pl.program_id(0)
     for s in range(grad_ref.shape[0]):
         left, right = left_ref[0, s].astype(BF16), right_ref[0, s].astype(BF16)
-        turned = dot_nn(dot_tn(left, grad_ref[s].astype(BF16)).astype(BF16), right)
+        grad = grad_ref[s]
+        turned = dot_nn(dot_tn(left, grad.astype(BF16)).astype(BF16), right)
         first = MOMENT_DECAY * first_ref[0, s] + (1.0 - MOMENT_DECAY) * turned
         second = MOMENT_DECAY * second_ref[0, s] + (1.0 - MOMENT_DECAY) * turned * turned
         stepped = first / (jnp.sqrt(second) + EPS_ADAM)
         back = dot_nt(dot_nn(left, stepped.astype(BF16)).astype(BF16), right)
         new = master_ref[0, s] - LEARN_RATE * back
+        wg_ref[0, s] = grad
         new_ref[0, s] = new
         nf_ref[0, s] = first
         ns_ref[0, s] = second
         low_ref[0, s] = new.astype(BF16)
 
-
-def update_blocks(grads, masters, first, second, left, right):
-    spd, edge = grads.shape[0], grads.shape[-1]
-    group = 2 if spd % 2 == 0 else 1
-    spec = pl.BlockSpec((1, group, edge, edge), lambda i: (0, i, 0, 0))
+    @pl.when(step == 0)
+    def _():
+        layer_ref[...] = layer_own[...]
+        input_ref[...] = input_own[...]
+        pieces = (2 * D + FF) // split_ref.shape[1]
+        head_w, ffn_w = D // pieces, FF // pieces
+        wide = jnp.concatenate([vec_ref[8 + i : 9 + i] for i in range(FF // D)], axis=1)
+        grad = jnp.zeros(split_ref.shape, F32)
+        for i in range(pieces):
+            mine = jnp.concatenate(
+                [
+                    vec_ref[6:7, i * head_w : (i + 1) * head_w],
+                    vec_ref[7:8, i * head_w : (i + 1) * head_w],
+                    wide[:, i * ffn_w : (i + 1) * ffn_w],
+                ],
+                axis=1,
+            )
+            grad = jnp.where(piece[0] == i, mine, grad)
+        adam(grad, sf_ref[...], ss_ref[...], split_ref[...], vec_outs[:4])
+        adam(vec_ref[0:6], rf_ref[...], rs_ref[...], row_ref[...], vec_outs[4:])
+
+    @pl.when(step == 1)
+    def _():
+        layer_ref[...] = layer_other[...]
+        input_ref[...] = input_other[...].astype(F32)
+
+
+def update_all(piece, owned, blocks, halves, summed, vectors):
+    masters = blocks[0]
+    spd, edge = masters.shape[1], masters.shape[-1]
+    group = spd // 2
+    whole = lambda a: pl.BlockSpec(a.shape, lambda i, p: tuple(0 for _ in a.shape))
+    spec = pl.BlockSpec((1, group, edge, edge), lambda i, p: (0, i, 0, 0))
+    half = pl.BlockSpec(halves[0].shape, lambda i, p: ((p[0] + i) % 2, 0))
+    shape = jax.ShapeDtypeStruct
+    vec_shapes = [shape(vectors[0].shape, F32)] * 4 + [shape(vectors[3].shape, F32)] * 4
+    total = 2 * halves[0].shape[0]
     return pl.pallas_call(
         update_kernel,
-        grid=(spd // group,),
-        in_specs=[pl.BlockSpec((group, edge, edge), lambda i: (i, 0, 0))] + [spec] * 5,
-        out_specs=[spec] * 4,
-        out_shape=[jax.ShapeDtypeStruct(masters.shape, F32)] * 3 + [jax.ShapeDtypeStruct(masters.shape, BF16)],
+        grid_spec=pltpu.PrefetchScalarGridSpec(
+            num_scalar_prefetch=1,
+            grid=(2,),
+            in_specs=[pl.BlockSpec((group, edge, edge), lambda i, p: (i, 0, 0))]
+            + [spec] * 5
+            + [whole(a) for a in (*halves, summed, *vectors)],
+            out_specs=[spec] * 5 + [half, half] + [whole(a) for a in vec_shapes],
+        ),
+        out_shape=[shape(masters.shape, F32)] * 4
+        + [shape(masters.shape, BF16), shape((total, D), BF16), shape((total, D), F32)]
+        + vec_shapes,
         compiler_params=params(),
         name="update",
-    )(grads, masters, first, second, left, right)
+    )(piece, owned, *blocks, *halves, summed, *vectors)
 
 
 def body(
@@ -799,69 +883,32 @@
 ):
     pieces = lax.axis_size("tensor")
     piece = lax.axis_index("tensor")
-    piece_width = HEADS * HEAD // pieces
-    piece_ffn = FF // pieces
-    block_edge = masters.shape[-1]
-    block_total = sum(block_counts(block_edge, piece_width, piece_ffn))
+    n_dp = lax.axis_size("dp")
     slots = block_of_slot.shape[0]
     full_seq = tokens.shape[0] // pair_lengths.shape[0]
     row_count = pair_lengths.shape[0] // pieces
-    n_dp = lax.axis_size("dp")
-    every, split_all = gather_all(masters[0].astype(BF16), split_vec, n_dp, pieces, pl.ANY)
-    slot_of = slot_table(block_of_slot, block_total)
     order = np.array(sum(block_home(pieces), []), np.int32)
-    homes = slot_of[order[:, 1]] + order[:, 0] * slots
-    query_bias = split_all[:, :piece_width].reshape(1, -1)
-    value_bias = split_all[:, piece_width : 2 * piece_width].reshape(1, -1)
-    up_bias = split_all[:, 2 * piece_width :].reshape(1, -1)
-    layer_own, input_own, grads, row_local, up_grad, qv_grad = layer_passes(
+    slot_numbers = jnp.arange(slots, dtype=jnp.int32)[:, None] + order[None, :, 0] * slots
+    homes = jnp.sum(jnp.where(block_of_slot[:, None] == order[None, :, 1], slot_numbers, 0), axis=0)
+    grads_at = np.array(grad_order(pieces), np.int32)
+    number = np.array([np.where(grads_at[:, 0] == i, grads_at[:, 1], -1) for i in range(pieces)])
+    index = jnp.arange(1, len(grads_at) + 1, dtype=jnp.int32)[None, :, None]
+    places = jnp.sum(jnp.where(number[:, :, None] == block_of_slot[None, None, :], index, 0), axis=1) - 1
+    every, query_bias, value_bias, up_bias = gather_all(masters, split_vec, n_dp, pieces)
+    layer_own, layer_other, input_own, input_other, grads, row_local, up_grad, qv_grad = layer_passes(
         tokens, cotangent, pair_lengths, piece, homes, every, query_bias, value_bias, up_bias, row_vec, row_count, full_seq
     )
-    layer_out = lax.all_gather(layer_own, "tensor", axis=0, tiled=True)
-    input_grad = lax.all_gather(input_own, "tensor", axis=0, tiled=True).astype(F32)
-    place_table = np.full((pieces, block_total + 1), -1, np.int32)
-    for index, (at_piece, number) in enumerate(grad_order(pieces)):
-        place_table[at_piece, number] = index
-    places = jnp.asarray(place_table)[:, block_of_slot].reshape(-1)
-    split_local = jnp.concatenate(
-        [
-            qv_grad[0].reshape(pieces, piece_width),
-            qv_grad[1].reshape(pieces, piece_width),
-            up_grad.reshape(pieces, piece_ffn),
-        ],
-        axis=1,
+    mean_scale = 1.0 / (tokens.shape[0] * n_dp)
+    owned, summed = scatter_all(places, grads, row_local, qv_grad, up_grad, n_dp, mean_scale)
+    outs = update_all(
+        piece.astype(jnp.int32).reshape(1),
+        owned,
+        (masters, mom_first, mom_second, left_bases, right_bases),
+        (layer_own, layer_other, input_own, input_other),
+        summed,
+        (split_vec, split_first, split_second, row_vec, row_first, row_second),
     )
-    mean_scale = 1.0 / (tokens.shape[0] * n_dp)
-    vectors = jnp.concatenate([split_local.reshape(-1, LANES), row_local.reshape(-1, LANES)], axis=0)
-    owned, summed = scatter_all(places, grads, vectors, n_dp, mean_scale)
-    weight_grads = owned[None]
-    split_rows = split_local.size // LANES
-    split_grad = lax.dynamic_slice_in_dim(summed[:split_rows].reshape(pieces, -1), piece, 1, 0)
-    row_grad = summed[split_rows:].reshape(row_local.shape)
-    new_masters, new_first, new_second, copies = update_blocks(
-        owned, masters, mom_first, mom_second, left_bases, right_bases
-    )
-    new_split, new_split_first, new_split_second = adam_vector(
-        split_grad, split_first, split_second, split_vec
-    )
-    new_row, new_row_first, new_row_second = adam_vector(row_grad, row_first, row_second, row_vec)
-    return (
-        layer_out,
-        input_grad,
-        weight_grads,
-        new_masters,
-        new_first,
-        new_second,
-        copies,
-        split_grad,
-        new_split,
-        new_split_first,
-        new_split_second,
-        row_grad,
-        new_row,
-        new_row_first,
-        new_row_second,
-    )
+    return (outs[5], outs[6], *outs[:5], *outs[7:])
 
 
 def solution(mesh):

time: 343 us -> 316 us (0.921)
  local copies, waits for them, and re-layouts: 14.9 us -> 1.17 us
  between operations: 14.3 us -> 0.92 us
  other arithmetic: 11.8 us -> 2.42 us
  Pallas kernels: 300 us -> 308 us
    convert_element_type x2 -> x0, other arithmetic: 7.11 us -> none  [the longest x1 5.08 us: body(): lax.all_gather(input_own, 'tensor', axis=0, tiled=True).astype(F32)]
    unnamed x33 -> x8, local copies, waits for them, and re-layouts: 8.01 us -> 1.17 us
    gather x3 -> x0, local copies, waits for them, and re-layouts: 4.83 us -> none  [the longest x1 3.15 us: body(): homes = slot_of[order[:, 1]] + order[:, 0] * slots]
    pallas_call x1, Pallas kernels: 96.5 us -> 101 us  [scatter_all(): pl.pallas_call(functools.partial(scatter_kernel, n_dp, spd, scale), in_sp...]
    pallas_call x2, Pallas kernels: 77.2 us -> 81 us  [the longest x1 68.2 us: gather_all(): pl.pallas_call(functools.partial(gather_kernel, n_dp, spd), in_specs=[vme...]
  transfers between devices with their start and end apart: 2 -> 2, of which waited for: 0 -> 0; matrix products, arithmetic and copies ran while one was open for 3% -> 0% of each run, Pallas kernels for 38% -> 39%
where the time goes in v4:
time: 316 us; the launch traced here: 315 us
  Pallas kernels  308 us (97%)
    pallas_call x1, Pallas kernels, scatter_all(): pl.pallas_call(functools.partial(scatter_kernel, n_dp, spd, scale), in_sp...  101 us
    pallas_call x1, Pallas kernels, gather_all(): pl.pallas_call(functools.partial(gather_kernel, n_dp, spd), in_specs=[vme...  68.2 us
    pallas_call x1, Pallas kernels, layer_passes(): pl.pallas_call(lambda homes, off, *refs: token_kernel(homes, *refs), grid...  48.1 us
    pallas_call x1, Pallas kernels, layer_passes(): pl.pallas_call(attend_back_kernel, grid_spec=pltpu.PrefetchScalarGridSpec...  30.2 us
    pallas_call x1, Pallas kernels, layer_passes(): pl.pallas_call(attend_kernel, grid_spec=pltpu.PrefetchScalarGridSpec(num_...  24.6 us
    pallas_call x1, Pallas kernels, layer_passes(): pl.pallas_call(lambda pc, *refs: grad_kernel(*refs), grid_spec=pltpu.Pref...  22.9 us
    pallas_call x1, Pallas kernels, update_all(): pl.pallas_call(update_kernel, grid_spec=pltpu.PrefetchScalarGridSpec(num_...  12.8 us
  transfers between devices with their start and end apart: 2, of which 0 were waited for; matrix products, arithmetic and copies ran while one was open for 0% of the time, Pallas kernels for 39%

profile of v4, /device:TPU:0, one launch (start us, length us, event | category | flops | bytes accessed | tf_op | source)
XLA Modules:
  0.0 314.5 jit_solution(4720328417360420757)
XLA Ops:
  0.6 68.2 %gather.1 = (bf16[448,128,128]{2,1,0:T(8,128)(2,1)}, f32[1,768]{1,0:T(1,128)}, f32[1,768]{1,0:T(1,128)}, f32[1,3072]{1,0:T(1,128)}) custom-call(f32[1,14,128,128]{3,2,1,0:T(8,128)} %master_ref.3, f32[1,2304]{1,0:T(1,128)} %split_ref.1), custom_call_target="tpu_custom_call" | custom-call | tf_op jit(solution)/shard_map/gather/pallas_call | solution.py:612
  68.8 1.6 select_reduce_fusion.1.homes
  70.4 24.6 %attend.1 = (bf16[18,1024,128]{2,1,0:T(8,128)(2,1)}, bf16[6,1024,128]{2,1,0:T(8,128)(2,1)}, f32[2,12,1,512]{3,2,1,0:T(1,128)}) custom-call(s32[432]{0:T(512)} %select_reduce_fusion.1.homes, s32[4,4]{1,0:T(4,128)} %pairs.3, s32[1]{0:T(128)} %bitcast.1.offset.off, bf16[2048,768]{1,0:T(8,128)(2,1)} %refs_4_.1, ...), custom_call_target="tpu_custom_call" | custom-call | flops 14495514624 | bytes 25165824 | tf_op jit(solution)/shard_map/attend/pallas_call | solution.py:365
  95.0 48.1 %tokenwise.1 = (bf16[1024,768]{1,0:T(8,128)(2,1)}, bf16[6,1024,128]{2,1,0:T(8,128)(2,1)}, bf16[24,1024,128]{2,1,0:T(8,128)(2,1)}, bf16[6,1024,128]{2,1,0:T(8,128...) custom-call(s32[432]{0:T(512)} %select_reduce_fusion.1.homes, ...), custom_call_target="tpu_custom_call" | custom-call | flops 24159191040 | bytes 50331648 | tf_op jit(solution)/shard_map/tokenwise/pallas_call | solution.py:387
  143.1 0.0 copy-start
  143.1 0.0 copy-start.2
  143.2 0.0 copy-start.3
  143.2 30.2 %attend_back.1 = (bf16[18,1024,128]{2,1,0:T(8,128)(2,1)}, f32[1024,768]{1,0:T(8,128)}, bf16[1024,768]{1,0:T(8,128)(2,1)}, f32[2,768]{1,0:T(2,128)}) custom-call(s32[432]{0:T(512)} %select_reduce_fusion.1.homes, s32[4,4]{1,0:T(4,128)} %pairs.3, s32[1]{0:T(128)} %bitcast.1.offset.off, bf16[18,1024,128]{2,1,0:T(8,128)(2,1)} %get-tuple-element.62.qkv_ref, ...), custom_call_target="tpu_custom_call" | custom-call | flops 19327352832 | bytes 31457280 | tf_op jit(solution)/shard_map/attend_back/pallas_call | solution.py:424
  173.4 0.8 collective-permute-start.1
  174.2 0.0 copy-done
  174.2 1.3 collective-permute-start
  175.5 0.0 copy-done.2
  175.5 0.0 copy-done.3
  175.5 0.3 select_reduce_fusion
  175.7 0.6 broadcast_add_fusion.places
  176.3 22.9 %weight_grads.1.g_ref = bf16[432,128,128]{2,1,0:T(8,128)(2,1)} custom-call(s32[1]{0:T(128)} %bitcast.pc.piece, bf16[24,1024,128]{2,1,0:T(8,128)(2,1)} %get-tuple-element.58.refs_0_, bf16[6,1024,128]{2,1,0:T(8,128)(2,1)} %get-tuple-element.59.refs_1_, bf16[6,1024,128]{2,1,0:T(8,128)(2,1)} %get-tuple-element.60.refs_2_, ...), custom_call_target="tpu_custom_call" | custom-call | flops 14495514624 | bytes 31457280 | tf_op jit(solution)/shard_map/weight_grads/pallas_call | solution.py:451
  199.2 101.1 %scatter.1 = (f32[14,128,128]{2,1,0:T(8,128)}, f32[16,768]{1,0:T(8,128)}) custom-call(s32[2,224]{1,0:T(2,128)} %broadcast_add_fusion.places, bf16[432,128,128]{2,1,0:T(8,128)(2,1)} %weight_grads.1.g_ref, f32[6,768]{1,0:T(8,128)} %get-tuple-element.68.rg_ref, f32[2,768]{1,0:T(2,128)} %get-tuple-element.69.sg_ref, f32[1,3072]{1,0:T(1,128)} %get-tuple-element.70.bg_ref), custom_call_target="tpu_custom_call" | custom-call | tf_op jit(solution)/shard_map/scatter/pallas_call | solution.py:757
  300.3 0.0 collective-permute-done.1.input_other
  300.3 0.0 copy-start.1
  300.4 0.0 collective-permute-done.layer_other
  300.4 1.2 copy-done.1
  301.5 12.8 %update.1 = (f32[1,14,128,128]{3,2,1,0:T(8,128)}, f32[1,14,128,128]{3,2,1,0:T(8,128)}, f32[1,14,128,128]{3,2,1,0:T(8,128)}, f32[1,14,128,128]{3,2,1,0:T(8,128)},...) custom-call(s32[1]{0:T(128)} %bitcast.pc.piece, ...), custom_call_target="tpu_custom_call" | custom-call | tf_op jit(solution)/shard_map/update/pallas_call | solution.py:849
  (1 shorter events, 0.0 us)
Async XLA Ops:
  143.1 31.1 %copy-start = (bf16[1024,768]{1,0:T(8,128)(2,1)S(1)}, bf16[1024,768]{1,0:T(8,128)(2,1)}, u32[]{:S(2)}) copy-start(bf16[1024,768]{1,0:T(8,128)(2,1)} %get-tuple-element.72.layer_own) | copy-start | bytes 4718596
  143.1 32.3 %copy-start.2 = (s32[224]{0:T(256)S(1)}, s32[224]{0:T(256)}, u32[]{:S(2)}) copy-start(s32[224]{0:T(256)} %param.21) | copy-start | bytes 2692
  143.2 32.3 %copy-start.3 = (s32[2,432]{1,0:T(2,128)S(1)}, s32[2,432]{1,0:T(2,128)}, u32[]{:S(2)}) copy-start(s32[2,432]{1,0:T(2,128)} %constant.31) | copy-start | bytes 10372
  173.4 127.0 %collective-permute-start.1 = (bf16[1024,768]{1,0:T(8,128)(2,1)}, bf16[1024,768]{1,0:T(8,128)(2,1)S(1)}, u32[]{:S(2)}, u32[]{:S(2)}) collective-permute-start(bf16[1024,768]{1,0:T(8,128)(2,1)} %get-tuple-element.74), channel_id=1, source_target_pairs={{0,1},{1,0},{2,3},{3,2},{4,5},{5,4},{6,7},{7,6},{8,9},{9,8},{10,11... | collective-permute-start | bytes 4718600 | tf_op jit(solution)/shard_map/ppermute | solution.py:447
  174.2 126.2 %collective-permute-start = (bf16[1024,768]{1,0:T(8,128)(2,1)S(1)}, bf16[1024,768]{1,0:T(8,128)(2,1)}, u32[]{:S(2)}, u32[]{:S(2)}) collective-permute-start(bf16[1024,768]{1,0:T(8,128)(2,1)S(1)} %copy-done), channel_id=1, source_target_pairs={{0,1},{1,0},{2,3},{3,2},{4,5},{5,4},{6,7},{7,6},{8,9},{9,8},{10,11... | collective-permute-start | bytes 4718600 | tf_op jit(solution)/shard_map/ppermute | solution.py:423
  300.3 1.2 copy-start.1

commit v5 on v4

--- a/solution.py
+++ b/solution.py
@@ -449,12 +449,12 @@
     part = lambda n: pl.BlockSpec((n, total, LANES), lambda j, *_: (j, 0, 0))
     blocks = 2 * f_s * d_b + 4 * d_b
     grads = pl.pallas_call(
-        lambda pc, *refs: grad_kernel(*refs),
+        lambda pc, wait, *refs: grad_kernel(*refs),
         grid_spec=pltpu.PrefetchScalarGridSpec(
             num_scalar_prefetch=1,
             grid=(d_b,),
             in_specs=[
-                part(f_s), whole((d_b, total, LANES)), whole((d_b, total, LANES)), part(f_s),
+                anywhere(), part(f_s), whole((d_b, total, LANES)), whole((d_b, total, LANES)), part(f_s),
                 pl.BlockSpec((total, D), lambda j, pc: (pc[0], 0)),
                 part(3), part(1), whole((d_b, total, LANES)),
             ],
@@ -464,23 +464,39 @@
         compiler_params=params(),
         cost_estimate=pl.CostEstimate(flops=24 * total * D * D, bytes_accessed=40 * total * D, transcendentals=0),
         name="weight_grads",
-    )(piece.astype(jnp.int32).reshape(1), active_low, down_low, normed_low, up_low, tokens, merged, att, attn_low)
+    )(piece.astype(jnp.int32).reshape(1), layer_other, active_low, down_low, normed_low, up_low, tokens, merged, att, attn_low)
     return layer_own, layer_other, input_own, input_other, grads, row_grad, up_grad, split_grad
 
 
-def bit_orders(n_dp, spd):
-    dp_bits = list(range(1, n_dp.bit_length() - 1))
-    near, far = dp_bits[:1], dp_bits[1:]
-    third = spd * 4 // 14
-    first = (spd - third) // 2
-    counts = (first, spd - third - first, third)
-    orders = ([-1] + near + far, near + [-1] + far, far + [-1] + near)
+def split_slots(orders, counts):
     parts, at = [], 0
     for order, count in zip(orders, counts):
         if count:
             parts.append((order, at, count))
         at += count
     return parts
+
+
+def index_bits(n_dp):
+    dp_bits = list(range(1, n_dp.bit_length() - 1))
+    return dp_bits[:1], dp_bits[1:]
+
+
+def gather_orders(n_dp, spd):
+    near, far = index_bits(n_dp)
+    third = spd * 4 // 14
+    first = (spd - third) // 2
+    return split_slots(
+        ([-1] + near + far, near + [-1] + far, far + [-1] + near), (first, spd - third - first, third)
+    )
+
+
+def scatter_orders(n_dp, spd):
+    near, far = index_bits(n_dp)
+    first, third = spd * 4 // 14, spd * 2 // 14
+    return split_slots(
+        ([-1] + far + near, near + [-1] + far, far + near + [-1]), (first, spd - third - first, third)
+    )
 
 
 def bit_of(number, bit):
@@ -533,7 +549,7 @@
 
 
 def gather_kernel(n_dp, spd, master_ref, vec_ref, all_ref, qb_ref, vb_ref, bu_ref, own_ref, both_ref, local_sem, send_sem, recv_sem, core_send, core_recv, vec_send, vec_recv):
-    parts = bit_orders(n_dp, spd)
+    parts = gather_orders(n_dp, spd)
     n_bits = len(parts[0][0])
     core = bit_of(lax.axis_index("dp"), 0)
     tensor = lax.axis_index("tensor")
@@ -604,7 +620,7 @@
 
 def gather_all(masters, vec, n_dp, pieces):
     spd, edge = masters.shape[1], masters.shape[-1]
-    parts = bit_orders(n_dp, spd)
+    parts = gather_orders(n_dp, spd)
     n, n_bits = len(parts), len(parts[0][0])
     dma = pltpu.SemaphoreType.DMA
     vmem = pl.BlockSpec(memory_space=pltpu.VMEM)
@@ -635,7 +651,7 @@
     give_ref, sum_ref, in_ref, vec_sum, vec_in,
     core_send, core_recv, send_sem, recv_sem, vec_send, vec_recv,
 ):
-    parts = bit_orders(n_dp, spd)
+    parts = scatter_orders(n_dp, spd)
     n_bits = len(parts[0][0])
     codes = 1 << n_bits
     core = bit_of(lax.axis_index("dp"), 0)
@@ -693,6 +709,8 @@
         return carry
 
     lax.fori_loop(0, ahead, first_hands, 0)
+    vec_step(0)
+    stage = 1
 
     def total_of(p, code, level, finish):
         order, at, count = parts[p]
@@ -723,11 +741,23 @@
                 passed(p, level, code).start()
             return carry
 
-        lax.fori_loop(0, 1 << level, onward, 0)
-        vec_step(n_bits - 1 - level)
+        count = 1 << level
+        if level == n_bits - 1 and count >= 4:
+            lax.fori_loop(0, 1, onward, 0)
+            vec_step(1)
+            lax.fori_loop(1, 3, onward, 0)
+            vec_step(2)
+            lax.fori_loop(3, count, onward, 0)
+            stage = 3
+        else:
+            lax.fori_loop(0, count, onward, 0)
+        if stage < n_bits:
+            vec_step(stage)
+            stage += 1
     for p in range(len(parts)):
         total_of(p, 0, -1, True)
-    vec_step(n_bits)
+    for last in range(stage, n_bits + 1):
+        vec_step(last)
     for stage in range(len(vec_bits)):
         vec_copy(stage).wait_send()
 
@@ -749,7 +779,7 @@
 def scatter_all(places, grads, row_grad, qv_grad, up_grad, n_dp, scale):
     edge = grads.shape[-1]
     spd = places.shape[1] // n_dp
-    parts = bit_orders(n_dp, spd)
+    parts = scatter_orders(n_dp, spd)
     n, n_bits = len(parts), len(parts[0][0])
     codes = 1 << n_bits
     dma = pltpu.SemaphoreType.DMA

time: 316 us -> 286 us (0.905)
  Pallas kernels: 308 us -> 273 us
  waiting for transfers between devices: 0.01 us -> 4.3 us
    pallas_call x1, Pallas kernels: 101 us -> 66.3 us  [scatter_all(): pl.pallas_call(functools.partial(scatter_kernel, n_dp, spd, scale), in_sp...]
    ppermute x1, waiting for transfers between devices: 0.01 us -> 4.3 us  [layer_passes(): layer_other = lax.ppermute(layer_own, 'tensor', swap)]
  transfers between devices with their start and end apart: 2 -> 2, of which waited for: 0 -> 1; matrix products, arithmetic and copies ran while one was open for 0% -> 0% of each run, Pallas kernels for 39% -> 42%
where the time goes in v5:
time: 286 us; the launch traced here: 285 us
  Pallas kernels  273 us (95%)
  waiting for transfers between devices  4.3 us (2%)
    pallas_call x1, Pallas kernels, gather_all(): pl.pallas_call(functools.partial(gather_kernel, n_dp, spd), in_specs=[vme...  68.2 us
    pallas_call x1, Pallas kernels, scatter_all(): pl.pallas_call(functools.partial(scatter_kernel, n_dp, spd, scale), in_sp...  66.3 us
    pallas_call x1, Pallas kernels, layer_passes(): pl.pallas_call(lambda homes, off, *refs: token_kernel(homes, *refs), grid...  48.2 us
    pallas_call x1, Pallas kernels, layer_passes(): pl.pallas_call(attend_back_kernel, grid_spec=pltpu.PrefetchScalarGridSpec...  30.2 us
    pallas_call x1, Pallas kernels, layer_passes(): pl.pallas_call(attend_kernel, grid_spec=pltpu.PrefetchScalarGridSpec(num_...  24.6 us
    pallas_call x1, Pallas kernels, layer_passes(): pl.pallas_call(lambda pc, wait, *refs: grad_kernel(*refs), grid_spec=pltp...  22.9 us
    pallas_call x1, Pallas kernels, update_all(): pl.pallas_call(update_kernel, grid_spec=pltpu.PrefetchScalarGridSpec(num_...  12.8 us
  transfers between devices with their start and end apart: 2, of which 1 were waited for; matrix products, arithmetic and copies ran while one was open for 0% of the time, Pallas kernels for 42%

profile of v5, /device:TPU:0, one launch (start us, length us, event | category | flops | bytes accessed | tf_op | source)
XLA Modules:
  0.0 285.2 jit_solution(8491812902851923636)
XLA Ops:
  0.6 68.2 %gather.1 = (bf16[448,128,128]{2,1,0:T(8,128)(2,1)}, f32[1,768]{1,0:T(1,128)}, f32[1,768]{1,0:T(1,128)}, f32[1,3072]{1,0:T(1,128)}) custom-call(f32[1,14,128,128]{3,2,1,0:T(8,128)} %master_ref.3, f32[1,2304]{1,0:T(1,128)} %split_ref.1), custom_call_target="tpu_custom_call" | custom-call | tf_op jit(solution)/shard_map/gather/pallas_call | solution.py:628
  68.8 1.6 select_reduce_fusion.1.homes
  70.4 24.6 %attend.1 = (bf16[18,1024,128]{2,1,0:T(8,128)(2,1)}, bf16[6,1024,128]{2,1,0:T(8,128)(2,1)}, f32[2,12,1,512]{3,2,1,0:T(1,128)}) custom-call(s32[432]{0:T(512)} %select_reduce_fusion.1.homes, s32[4,4]{1,0:T(4,128)} %pairs.3, s32[1]{0:T(128)} %bitcast.1.offset.off, bf16[2048,768]{1,0:T(8,128)(2,1)} %refs_4_.1, ...), custom_call_target="tpu_custom_call" | custom-call | flops 14495514624 | bytes 25165824 | tf_op jit(solution)/shard_map/attend/pallas_call | solution.py:365
  95.0 48.2 %tokenwise.1 = (bf16[1024,768]{1,0:T(8,128)(2,1)}, bf16[6,1024,128]{2,1,0:T(8,128)(2,1)}, bf16[24,1024,128]{2,1,0:T(8,128)(2,1)}, bf16[6,1024,128]{2,1,0:T(8,128...) custom-call(s32[432]{0:T(512)} %select_reduce_fusion.1.homes, ...), custom_call_target="tpu_custom_call" | custom-call | flops 24159191040 | bytes 50331648 | tf_op jit(solution)/shard_map/tokenwise/pallas_call | solution.py:387
  143.2 0.8 collective-permute-start
  144.0 0.0 copy-start.2
  144.0 0.0 copy-start.3
  144.0 30.2 %attend_back.1 = (bf16[18,1024,128]{2,1,0:T(8,128)(2,1)}, f32[1024,768]{1,0:T(8,128)}, bf16[1024,768]{1,0:T(8,128)(2,1)}, f32[2,768]{1,0:T(2,128)}) custom-call(s32[432]{0:T(512)} %select_reduce_fusion.1.homes, s32[4,4]{1,0:T(4,128)} %pairs.3, s32[1]{0:T(128)} %bitcast.1.offset.off, bf16[18,1024,128]{2,1,0:T(8,128)(2,1)} %get-tuple-element.63.qkv_ref, ...), custom_call_target="tpu_custom_call" | custom-call | flops 19327352832 | bytes 31457280 | tf_op jit(solution)/shard_map/attend_back/pallas_call | solution.py:424
  174.2 1.3 collective-permute-start.1
  175.5 0.0 copy-done.2
  175.5 0.0 copy-done.3
  175.5 0.3 select_reduce_fusion
  175.8 0.6 broadcast_add_fusion.places
  176.4 4.3 %collective-permute-done.wait.layer_other = bf16[1024,768]{1,0:T(8,128)(2,1)S(1)} collective-permute-done((bf16[1024,768]{1,0:T(8,128)(2,1)}, bf16[1024,768]{1,0:T(8,128)(2,1)S(1)}, u32[]{:S(2)}, u32[]{:S(2)}) %collective-permute-start) | collective-permute-done | bytes 1572896 | tf_op jit(solution)/shard_map/ppermute | solution.py:423
  180.7 0.0 copy-start
  180.7 1.2 copy-done
  181.8 22.9 %weight_grads.1.g_ref = bf16[432,128,128]{2,1,0:T(8,128)(2,1)} custom-call(s32[1]{0:T(128)} %bitcast.pc.piece, bf16[1024,768]{1,0:T(8,128)(2,1)} %copy-done, bf16[24,1024,128]{2,1,0:T(8,128)(2,1)} %get-tuple-element.59.refs_0_, bf16[6,1024,128]{2,1,0:T(8,128)(2,1)} %get-tuple-element.60.refs_1_, bf16[6,1024,128]{2,1,0:T(8,128)(2,1)} %get-tuple-element.61.refs_2_, ...), custom_call_target="tpu_custom_call" | custom-call | flops 14495514624 | bytes 31457280 | tf_op jit(solution)/shard_map/weight_grads/pallas_call | solution.py:451
  204.7 66.3 %scatter.1 = (f32[14,128,128]{2,1,0:T(8,128)}, f32[16,768]{1,0:T(8,128)}) custom-call(s32[2,224]{1,0:T(2,128)} %broadcast_add_fusion.places, bf16[432,128,128]{2,1,0:T(8,128)(2,1)} %weight_grads.1.g_ref, f32[6,768]{1,0:T(8,128)} %get-tuple-element.69.rg_ref, f32[2,768]{1,0:T(2,128)} %get-tuple-element.70.sg_ref, f32[1,3072]{1,0:T(1,128)} %get-tuple-element.71.bg_ref), custom_call_target="tpu_custom_call" | custom-call | tf_op jit(solution)/shard_map/scatter/pallas_call | solution.py:787
  271.0 0.0 collective-permute-done.1.input_other
  271.0 0.0 copy-start.1
  271.0 1.2 copy-done.1
  272.2 12.8 %update.1 = (f32[1,14,128,128]{3,2,1,0:T(8,128)}, f32[1,14,128,128]{3,2,1,0:T(8,128)}, f32[1,14,128,128]{3,2,1,0:T(8,128)}, f32[1,14,128,128]{3,2,1,0:T(8,128)},...) custom-call(s32[1]{0:T(128)} %bitcast.pc.piece, ...), custom_call_target="tpu_custom_call" | custom-call | tf_op jit(solution)/shard_map/update/pallas_call | solution.py:879
  (1 shorter events, 0.0 us)
Async XLA Ops:
  143.2 37.5 %collective-permute-start = (bf16[1024,768]{1,0:T(8,128)(2,1)}, bf16[1024,768]{1,0:T(8,128)(2,1)S(1)}, u32[]{:S(2)}, u32[]{:S(2)}) collective-permute-start(bf16[1024,768]{1,0:T(8,128)(2,1)} %get-tuple-element.58.layer_own), channel_id=1, source_target_pairs={{0,1},{1,0},{2,3},{3,2},{4,5},{5,4},{6,7},{7,6},{8,9},{9,8},{10,11... | collective-permute-start | bytes 4718600 | tf_op jit(solution)/shard_map/ppermute | solution.py:423
  144.0 31.5 %copy-start.2 = (s32[224]{0:T(256)S(1)}, s32[224]{0:T(256)}, u32[]{:S(2)}) copy-start(s32[224]{0:T(256)} %param.21) | copy-start | bytes 2692
  144.0 31.5 %copy-start.3 = (s32[2,432]{1,0:T(2,128)S(1)}, s32[2,432]{1,0:T(2,128)}, u32[]{:S(2)}) copy-start(s32[2,432]{1,0:T(2,128)} %constant.31) | copy-start | bytes 10372
  174.2 96.9 %collective-permute-start.1 = (bf16[1024,768]{1,0:T(8,128)(2,1)}, bf16[1024,768]{1,0:T(8,128)(2,1)S(1)}, u32[]{:S(2)}, u32[]{:S(2)}) collective-permute-start(bf16[1024,768]{1,0:T(8,128)(2,1)} %get-tuple-element.74), channel_id=1, source_target_pairs={{0,1},{1,0},{2,3},{3,2},{4,5},{5,4},{6,7},{7,6},{8,9},{9,8},{10,11... | collective-permute-start | bytes 4718600 | tf_op jit(solution)/shard_map/ppermute | solution.py:447
  180.7 1.2 copy-start
  271.0 1.2 copy-start.1
